TPU v7x, 32 devices: a whole 2x2x4 slice. The times are simulated.
32 devices in a mesh: rep: 2 (over x), ep: 16 (over z, y, core).
Axes of the slice: x: 2, y: 2, z: 4, core: 2. Of those that a mesh axis runs over, the one named last changes fastest.
Arguments:
- hidden_in: bfloat16 [4, 64, 7168], P(None, 'ep'), may hold values from -6 to 6
- queries: bfloat16 [4, 64, 8192], P(None, None, 'ep'), may hold values from -216 to 216
- new_keys: bfloat16 [4, 64, 8192], P(None, None, 'ep'), may hold values from -6 to 6
- new_values: bfloat16 [4, 64, 8192], P(None, None, 'ep'), may hold values from -6 to 6
- cache_keys: bfloat16 [64, 32, 8192], P(None, None, 'ep'), may hold values from -6 to 6
- cache_values: bfloat16 [64, 32, 8192], P(None, None, 'ep'), may hold values from -6 to 6
- cache_lengths: int32 [64], replicated, may hold values from 1 to 32, 1056 in all
- expert_ids: int32 [4, 64, 8], P(None, 'ep'), may hold values from 0 to 15, all different within a row; in each aligned block of 4 rows (0 to 3, 4 to 7, ..., all dimensions but the last counted through in order) at most 4 rows name the same one
- router_logits: float32 [4, 64, 8], P(None, 'ep'), may hold values from -6 to 6
- norm_gain: float32 [7168], replicated, may hold values from 0.1 to 1.9
- out_sectioned: bfloat16 [8192, 7168], P('ep', 'rep'), may hold values from -0.0625 to 0.0625
- expert_sectioned: bfloat16 [16, 7168, 3, 1024], P('ep', 'rep'), may hold values from -0.09375 to 0.09375
- bucket_owner: int32 [16, 2], P('ep'), may hold values from 0 to 1, each once within a row
Outputs:
- layer_out: bfloat16 [4, 64, 7168], P(None, 'ep')
Inputs may be any that keep to these rules, and one draw needn't show every extreme that they name: `expert_ids`: within one step, the rows of one device (aligned blocks of 4 rows) name no expert more than 4 times; some expert is named exactly 4 times. Each row names distinct experts. `bucket_owner`: for each expert the owners of its 2 buckets are distinct.
All inputs are finite; a program needn't handle non-finite values.
Results may differ from a plain program's by a relative error of at most 0.025.
Values may be sent and summed in bfloat16 or wider, within the bound.
A program may use at most 192 MiB of HBM per device.

v0:
```python
import math

import jax
import jax.numpy as jnp
from jax import lax
from jax.sharding import PartitionSpec as P

DH = 128


ROUTE_SCALE = 2.827
EPSILON = 1e-06


def attention(
    query_rows, key_cache, value_cache, fresh_keys, fresh_values, row_lengths, step_index, head_size
):
    row_count, feature_count = query_rows.shape
    head_count = feature_count // head_size
    cached = key_cache.shape[1]
    step_count = fresh_keys.shape[0]
    query_heads = query_rows.reshape(row_count, head_count, head_size)
    keys_old = key_cache.reshape(row_count, cached, head_count, head_size)
    values_old = value_cache.reshape(row_count, cached, head_count, head_size)
    keys_recent = fresh_keys.reshape(step_count, row_count, head_count, head_size)
    values_recent = fresh_values.reshape(step_count, row_count, head_count, head_size)
    factor = 1.0 / math.sqrt(head_size)
    scores_old = (
        jnp.einsum("rhd,rchd->rhc", query_heads, keys_old, preferred_element_type=jnp.float32)
        * factor
    )
    in_cache = jnp.arange(cached, dtype=jnp.int32)[None, :] < row_lengths[:, None]
    scores_old = jnp.where(in_cache[:, None, :], scores_old, -1e30)
    scores_recent = (
        jnp.einsum("rhd,srhd->rhs", query_heads, keys_recent, preferred_element_type=jnp.float32)
        * factor
    )
    visible = jnp.arange(step_count, dtype=jnp.int32) <= step_index
    scores_recent = jnp.where(visible[None, None, :], scores_recent, -1e30)
    scores = jnp.concatenate([scores_old, scores_recent], axis=2)
    largest = jnp.max(scores, axis=2, keepdims=True)
    expsum = jnp.exp(scores - largest)
    denominator = jnp.sum(expsum, axis=2)
    probs = expsum.astype(jnp.bfloat16)
    weighted = jnp.einsum(
        "rhc,rchd->rhd", probs[:, :, :cached], values_old, preferred_element_type=jnp.float32
    )
    weighted = weighted + jnp.einsum(
        "rhs,srhd->rhd", probs[:, :, cached:], values_recent, preferred_element_type=jnp.float32
    )
    return (
        (weighted / denominator[:, :, None]).astype(jnp.bfloat16).reshape(row_count, feature_count)
    )


def on_device(
    hidden_in,
    queries,
    new_keys,
    new_values,
    cache_keys,
    cache_values,
    cache_lengths,
    expert_ids,
    router_logits,
    norm_gain,
    out_sectioned,
    expert_sectioned,
    bucket_owner,
):
    step_count, row_block, model_width = hidden_in.shape
    all_rows = queries.shape[1]
    choose_count = expert_ids.shape[2]
    expert_ranks = lax.axis_size("ep")
    replica_ranks = lax.axis_size("rep")
    share_width = model_width // replica_ranks
    owners = bucket_owner[0]
    relaid = lax.all_to_all(expert_sectioned, "rep", split_axis=3, concat_axis=1, tiled=True)
    hidden_share = relaid.shape[3]
    row_blocks = relaid.reshape(replica_ranks, share_width, 3, hidden_share)
    expert_local = jnp.take(row_blocks, owners, axis=0).reshape(model_width, 3, hidden_share)
    gate_weight = expert_local[:, 0]
    up_weight = expert_local[:, 1]
    down_weight = expert_local[:, 2]
    head_list = [
        attention(
            queries[step_index],
            cache_keys,
            cache_values,
            new_keys,
            new_values,
            cache_lengths,
            step_index,
            DH,
        )
        for step_index in range(step_count)
    ]
    head_matrix = jnp.stack(head_list).reshape(step_count * all_rows, -1)
    partials = jnp.dot(
        head_matrix,
        lax.all_gather(out_sectioned, "rep", axis=1, tiled=True),
        preferred_element_type=jnp.float32,
    )
    head_total = lax.psum_scatter(
        partials.reshape(step_count, all_rows, model_width).astype(jnp.bfloat16),
        "ep",
        scatter_dimension=1,
        tiled=True,
    )
    residual = hidden_in.astype(jnp.float32) + head_total.astype(jnp.float32)
    mean_square = jnp.mean(residual * residual, axis=2, keepdims=True)
    normalized = (residual * lax.rsqrt(mean_square + EPSILON) * norm_gain).astype(jnp.bfloat16)
    capacity = min(row_block, max(2, 2 * all_rows * choose_count // (expert_ranks * expert_ranks)))
    chosen = expert_ids.reshape(step_count, row_block * choose_count)
    one_hot = (chosen[:, :, None] == jnp.arange(expert_ranks, dtype=jnp.int32)).astype(jnp.int32)
    earlier_count = jnp.sum((jnp.cumsum(one_hot, axis=1) - one_hot) * one_hot, axis=2)
    step_offset = jnp.arange(step_count, dtype=jnp.int32)[:, None] * capacity
    slot_order = (chosen * (step_count * capacity) + step_offset + earlier_count).reshape(-1)
    slot_count = expert_ranks * step_count * capacity
    placement = (jnp.arange(slot_count, dtype=jnp.int32)[:, None] == slot_order[None, :]).astype(
        jnp.bfloat16
    )
    repeated = jnp.repeat(
        normalized.reshape(step_count * row_block, model_width), choose_count, axis=0
    )
    outgoing = jnp.dot(placement, repeated, preferred_element_type=jnp.float32).astype(jnp.bfloat16)
    outgoing = outgoing.reshape(expert_ranks, step_count * capacity, model_width)
    parcel = lax.all_to_all(outgoing, "ep", split_axis=0, concat_axis=0, tiled=True)
    item_count = parcel.shape[1]
    arrivals = parcel.reshape(-1, model_width)
    gate_value = jnp.dot(arrivals, gate_weight, preferred_element_type=jnp.float32)
    up_value = jnp.dot(arrivals, up_weight, preferred_element_type=jnp.float32)
    activated = (jax.nn.silu(gate_value) * up_value).astype(jnp.bfloat16)
    expert_part = jnp.einsum(
        "nf,df->nd", activated, down_weight, preferred_element_type=jnp.float32
    )
    summed_share = lax.psum_scatter(
        expert_part.astype(jnp.bfloat16), "rep", scatter_dimension=1, tiled=True
    )
    finished = lax.all_gather(summed_share, "rep", axis=1, tiled=True)
    result = lax.all_to_all(
        finished.reshape(expert_ranks, item_count, model_width),
        "ep",
        split_axis=0,
        concat_axis=0,
        tiled=True,
    )
    affinity = jax.nn.sigmoid(router_logits)
    gate_share = ROUTE_SCALE * affinity / jnp.sum(affinity, axis=2, keepdims=True)
    owner_row = jnp.arange(step_count * row_block * choose_count, dtype=jnp.int32) // choose_count
    mixing = jnp.where(
        jnp.arange(step_count * row_block, dtype=jnp.int32)[:, None] == owner_row[None, :],
        gate_share.reshape(-1)[None, :],
        0.0,
    )
    selecting = (slot_order[:, None] == jnp.arange(slot_count, dtype=jnp.int32)[None, :]).astype(
        jnp.float32
    )
    combining = jnp.dot(mixing, selecting, precision=lax.Precision.HIGHEST)
    routed = jnp.dot(
        combining,
        result.reshape(slot_count, -1).astype(jnp.float32),
        precision=lax.Precision.HIGHEST,
    )
    layer_out = (residual + routed.reshape(step_count, row_block, model_width)).astype(jnp.bfloat16)
    return layer_out


def solution(mesh):
    return jax.shard_map(
        on_device,
        mesh=mesh,
        in_specs=(
            P(None, "ep", None),
            P(None, None, "ep"),
            P(None, None, "ep"),
            P(None, None, "ep"),
            P(None, None, "ep"),
            P(None, None, "ep"),
            P(),
            P(None, "ep", None),
            P(None, "ep", None),
            P(),
            P("ep", "rep"),
            P("ep", "rep", None, None),
            P("ep", None),
        ),
        out_specs=P(None, "ep", None),
        check_vma=False,
    )
```

profile of v0, /device:TPU:0, one launch (start us, length us, event | category | flops | bytes accessed | tf_op | source)
XLA Modules:
  0.0 818.7 jit_solution(6072759624118451464)
XLA Ops:
  7.3 47.8 %copy.44 = bf16[1,3584,3,1024]{1,2,0,3:T(4,128)(2,1)} copy(bf16[1,3584,3,1024]{3,1,2,0:T(8,128)(2,1)} %param.24) | data formatting | bytes 44040192 | tf_op args[11]
  55.1 12.6 %all-to-all-start.1 = ((bf16[1,3584,3,1024]{1,2,0,3:T(4,128)(2,1)}), bf16[1,3584,3,1024]{1,2,0,3:T(4,128)(2,1)}, u32[]{:S(2)}, u32[]{:S(2)}) async-start(bf16[1,3584,3,1024]{1,2,0,3:T(4,128)(2,1)} %copy.44), calls=%async_computation.1 | async-start | bytes 58720256 | tf_op jit(solution)/shard_map/all_to_all | solution.py:78
  92.3 43.6 %all-gather.3.cloned.1.call-done = bf16[512,7168]{1,0:T(8,128)(2,1)} async-done(((bf16[512,3584]{1,0:T(8,128)(2,1)}), bf16[512,7168]{1,0:T(8,128)(2,1)}) %all-gather.3.cloned.1.call-update) | async-done | bytes 7340048 | tf_op jit(solution)/shard_map/all_gather | solution.py:101
  135.9 7.2 convolution_convert_fusion.2
  145.4 104.6 %all-reduce.3.cloned.1.call-done = bf16[4,64,7168]{2,1,0:T(8,128)(2,1)} async-done(((bf16[4,64,7168]{2,1,0:T(8,128)(2,1)}), bf16[4,64,7168]{2,1,0:T(8,128)(2,1)}) %all-reduce.3.cloned.1.call-update) | async-done | bytes 3670032
  255.6 162.6 %all-to-all-done.1 = bf16[1,3584,3,1024]{1,2,0,3:T(4,128)(2,1)} async-done(((bf16[1,3584,3,1024]{1,2,0,3:T(4,128)(2,1)}), bf16[1,3584,3,1024]{1,2,0,3:T(4,128)(2,1)}, u32[]{:S(2)}, u32[]{:S(2)}) %all-to-all-start.1) | async-done | bytes 22020128 | tf_op jit(solution)/shard_map/all_to_all | solution.py:78
  418.3 5.7 all-to-all-start
  424.0 20.8 %fusion.109 = (bf16[1,3584,3,512]{1,2,0,3:T(4,128)(2,1)}, bf16[1,3584,3,512]{1,2,0,3:T(4,128)(2,1)}) fusion(bf16[1,3584,3,1024]{1,2,0,3:T(4,128)(2,1)} %all-to-all-done.1), kind=kLoop, calls=%fused_computation.172 | loop fusion | bytes 44040192 | tf_op jit(solution)/shard_map/slice
  444.8 21.9 %copy.96 = bf16[1,3584,3,512]{3,1,2,0:T(8,128)(2,1)} copy(bf16[1,3584,3,512]{1,2,0,3:T(4,128)(2,1)} %get-tuple-element.21) | data formatting | bytes 22020096
  466.8 21.9 %copy.97 = bf16[1,3584,3,512]{3,1,2,0:T(8,128)(2,1)} copy(bf16[1,3584,3,512]{1,2,0,3:T(4,128)(2,1)} %get-tuple-element.22) | data formatting | bytes 22020096
  488.7 12.0 %pad_maximum_fusion = bf16[1,7168,3,512]{3,1,2,0:T(8,128)(2,1)S(1)} fusion(bf16[1,3584,3,512]{3,1,2,0:T(8,128)(2,1)} %copy.97, bf16[1,3584,3,512]{3,1,2,0:T(8,128)(2,1)} %copy.96), kind=kLoop, calls=%fused_computation.7 | loop fusion | flops 44040192 | bytes 44040192 | tf_op jit(solution)/shard_map/concatenate
  500.7 7.3 copy-done.2
  508.2 12.8 %fusion.110 = (bf16[2,640,3,512]{3,1,0,2:T(8,128)(2,1)S(1)}, bf16[2,640,3,512]{3,1,0,2:T(8,128)(2,1)}, bf16[2,640,3,512]{3,1,0,2:T(8,128)(2,1)}, bf16[2,640,3,512]{3,1,0,2:T(8,128)(2,1)}, bf16[2,640,3,512]{3,1,0,2:T(8,128)(2,1)}) fusion(bf16[2,3584,3,512]{3,1,0,2:T(8,128)(2,1)} %bitcast.175), kind=kLoop, calls=%fused_computation.173 | loop fusion | bytes 39321600 | tf_op jit(solution)/shard_map/jit(_take)/gather | solution.py:81
  525.0 4.9 gather_fusion.4
  533.7 4.5 copy.101
  538.2 4.8 gather_fusion.3
  543.0 4.5 copy.100
  547.5 4.7 gather_fusion.2
  552.2 4.5 copy.99
  556.7 4.9 gather_fusion.1
  561.6 4.5 copy.98
  566.1 4.8 gather_fusion
  570.8 4.7 constant_dynamic-update-slice_fusion.5
  590.2 11.2 %copy.53 = bf16[2,3584,3,512]{3,1,0,2:T(8,128)(2,1)S(1)} copy(bf16[2,3584,3,512]{3,1,2,0:T(8,128)(2,1)} %constant_dynamic-update-slice_fusion) | data formatting | bytes 44040192
  601.4 10.8 %bitcast_select_fusion = bf16[7168,3,512]{2,0,1:T(8,128)(2,1)} fusion(bf16[2,3584,3,512]{3,1,0,2:T(8,128)(2,1)S(1)} %copy.53, pred[7168]{0:T(1024)(128)(4,1)S(1)} %broadcast_in_dim.130), kind=kLoop, calls=%fused_computation.8 | loop fusion | flops 11010048 | bytes 44047360 | tf_op jit(solution)/shard_map/jit(_take)/select_n | solution.py:81
  612.1 6.2 fusion.3
  618.4 6.3 fusion.31
  624.7 7.0 convolution_convert_fusion.1
  631.8 49.5 %reduce-scatter.3.cloned.1.call-done = bf16[256,3584]{1,0:T(8,128)(2,1)} async-done(((bf16[256,7168]{1,0:T(8,128)(2,1)}), bf16[256,3584]{1,0:T(8,128)(2,1)}) %reduce-scatter.3.cloned.1.call-update) | async-done | bytes 1835024 | tf_op jit(solution)/shard_map/reduce_scatter | solution.py:137
  681.4 52.2 %all-gather.5.cloned.1.call-done = bf16[256,7168]{1,0:T(8,128)(2,1)} async-done(((bf16[256,3584]{1,0:T(8,128)(2,1)}), bf16[256,7168]{1,0:T(8,128)(2,1)}) %all-gather.5.cloned.1.call-update) | async-done | bytes 3670032 | tf_op jit(solution)/shard_map/all_gather | solution.py:140
  733.6 5.7 all-to-all-start.2
  739.8 68.1 %all-to-all-done.2 = bf16[16,16,7168]{2,1,0:T(8,128)(2,1)} async-done(((bf16[16,16,7168]{2,1,0:T(8,128)(2,1)}), bf16[16,16,7168]{2,1,0:T(8,128)(2,1)}, u32[]{:S(2)}, u32[]{:S(2)}) %all-to-all-start.2) | async-done | bytes 3670048 | tf_op jit(solution)/shard_map/all_to_all | solution.py:141
  (158 shorter events, 59.8 us)
Async XLA Ops:
  6.5 80.6 %copy-start = (bf16[64,32,512]{2,1,0:T(8,128)(2,1)S(1)}, bf16[64,32,512]{2,1,0:T(8,128)(2,1)}, u32[]{:S(2)}) copy-start(bf16[64,32,512]{2,1,0:T(8,128)(2,1)} %param.18) | copy-start | bytes 6291460
  6.5 129.4 %all-gather.3.cloned.1.call-start = ((), (), s32[]{:S(2)}) async-start(), calls=%async_computation.4 | async-start | bytes 11010048 | tf_op jit(solution)/shard_map/all_gather | solution.py:101
  55.1 12.6 %copy-start.9 = (bf16[4,64,512]{2,1,0:T(8,128)(2,1)S(1)}, bf16[4,64,512]{2,1,0:T(8,128)(2,1)}, u32[]{:S(2)}) copy-start(bf16[4,64,512]{2,1,0:T(8,128)(2,1)} %param.15) | copy-start | bytes 786436
  55.1 12.7 %copy-start.10 = (bf16[4,64,512]{2,1,0:T(8,128)(2,1)S(1)}, bf16[4,64,512]{2,1,0:T(8,128)(2,1)}, u32[]{:S(2)}) copy-start(bf16[4,64,512]{2,1,0:T(8,128)(2,1)} %param.14) | copy-start | bytes 786436
  55.1 363.2 %all-to-all-start.1 = ((bf16[1,3584,3,1024]{1,2,0,3:T(4,128)(2,1)}), bf16[1,3584,3,1024]{1,2,0,3:T(4,128)(2,1)}, u32[]{:S(2)}, u32[]{:S(2)}) async-start(bf16[1,3584,3,1024]{1,2,0,3:T(4,128)(2,1)} %copy.44), calls=%async_computation.1 | async-start | bytes 58720256 | tf_op jit(solution)/shard_map/all_to_all | solution.py:78
  67.6 182.4 %all-reduce.3.cloned.1.call-start = ((), (), s32[]{:S(2)}) async-start(), calls=%async_computation.7 | async-start | bytes 7340032
  67.9 5.0 copy-start.15
  71.7 6.2 copy-start.11
  75.2 9.7 %copy-start.14 = (s32[64]{0:T(128)S(1)}, s32[64]{0:T(128)}, u32[]{:S(2)}) copy-start(s32[64]{0:T(128)} %param.19) | copy-start | bytes 772
  92.3 51.0 %copy-start.12 = (s32[4,4,8]{2,1,0:T(4,128)S(1)}, s32[4,4,8]{2,1,0:T(4,128)}, u32[]{:S(2)}) copy-start(s32[4,4,8]{2,1,0:T(4,128)} %param.20) | copy-start | bytes 1540
  92.3 51.2 %copy-start.17 = (s32[1,2]{1,0:T(1,128)S(1)}, s32[1,2]{1,0:T(1,128)}, u32[]{:S(2)}) copy-start(s32[1,2]{1,0:T(1,128)} %param.25) | copy-start | bytes 28
  143.1 1.0 copy-start.18
  143.1 106.9 %copy-start.8 = (bf16[4,4,7168]{2,1,0:T(4,128)(2,1)S(1)}, bf16[4,4,7168]{2,1,0:T(4,128)(2,1)}, u32[]{:S(2)}) copy-start(bf16[4,4,7168]{2,1,0:T(4,128)(2,1)} %param.13) | copy-start | bytes 688132
  143.1 108.3 %copy-start.13 = (f32[7168]{0:T(1024)S(1)}, f32[7168]{0:T(1024)}, u32[]{:S(2)}) copy-start(f32[7168]{0:T(1024)} %param.22) | copy-start | bytes 86020
  418.3 193.9 %all-to-all-start = ((bf16[16,16,7168]{2,1,0:T(8,128)(2,1)}), bf16[16,16,7168]{2,1,0:T(8,128)(2,1)}, u32[]{:S(2)}, u32[]{:S(2)}) async-start(bf16[16,16,7168]{2,1,0:T(8,128)(2,1)} %bitcast.176), calls=%async_computation | async-start | bytes 7340032 | tf_op jit(solution)/shard_map/all_to_all | solution.py:128
  423.9 257.4 %reduce-scatter.3.cloned.1.call-start = ((), (), s32[]{:S(2)}) async-start(), calls=%async_computation.5 | async-start | bytes 5505024 | tf_op jit(solution)/shard_map/reduce_scatter | solution.py:137
  500.7 7.3 copy-start.2
  570.8 4.7 copy-start.6
  575.5 3.5 copy-start.5
  579.0 3.5 copy-start.4
  582.6 3.5 copy-start.3
  586.1 2.4 copy-start.7
  631.7 101.9 %all-gather.5.cloned.1.call-start = ((), (), s32[]{:S(2)}) async-start(), calls=%async_computation.6 | async-start | bytes 5505024 | tf_op jit(solution)/shard_map/all_gather | solution.py:140
  681.4 57.9 %copy-start.16 = (f32[4,4,8]{2,1,0:T(4,128)S(1)}, f32[4,4,8]{2,1,0:T(4,128)}, u32[]{:S(2)}) copy-start(f32[4,4,8]{2,1,0:T(4,128)} %param.21) | copy-start | bytes 1540
  733.6 74.2 %all-to-all-start.2 = ((bf16[16,16,7168]{2,1,0:T(8,128)(2,1)}), bf16[16,16,7168]{2,1,0:T(8,128)(2,1)}, u32[]{:S(2)}, u32[]{:S(2)}) async-start(bf16[16,16,7168]{2,1,0:T(8,128)(2,1)} %bitcast.177), calls=%async_computation.3 | async-start | bytes 7340032 | tf_op jit(solution)/shard_map/all_to_all | solution.py:141
  739.3 72.9 %copy-start.1 = (bf16[64,32,512]{2,1,0:T(8,128)(2,1)S(1)}, bf16[64,32,512]{2,1,0:T(8,128)(2,1)}, u32[]{:S(2)}) copy-start(bf16[64,32,512]{2,1,0:T(8,128)(2,1)} %param.18) | copy-start | bytes 6291460
Sparse Core Ops, SparseCore 0:
  8.9 126.9 all-gather.2
  143.3 106.7 all-reduce.2
  631.9 49.4 reduce-scatter.2
  682.7 50.8 all-gather.4
where the time goes:
time: 834 us; the launch traced here: 819 us
  waiting for transfers between devices  481 us (58%)
  local copies, waits for them, and re-layouts  220 us (26%)
  matrix products  51.7 us (6%)
  other arithmetic  27.1 us (3%)
  starting transfers between devices  24 us (3%)
  between operations  14.4 us (2%)
    all_to_all x1, waiting for transfers between devices, on_device(): lax.all_to_all(expert_sectioned, 'rep', split_axis=3, concat_axis=1, tile...  163 us
    unnamed x55, local copies, waits for them, and re-layouts  152 us
    unnamed x5, waiting for transfers between devices  105 us
    all_to_all x1, waiting for transfers between devices, on_device(): lax.all_to_all(finished.reshape(expert_ranks, item_count, model_width), '...  68.1 us
    all_gather x1, waiting for transfers between devices, on_device(): finished = lax.all_gather(summed_share, 'rep', axis=1, tiled=True)  52.2 us
    reduce_scatter x1, waiting for transfers between devices, on_device(): lax.psum_scatter(expert_part.astype(jnp.bfloat16), 'rep', scatter_dimensi...  49.5 us
    all_gather x1, waiting for transfers between devices, on_device(): lax.all_gather(out_sectioned, 'rep', axis=1, tiled=True)  43.6 us
    gather x8, local copies, waits for them, and re-layouts, on_device(): jnp.take(row_blocks, owners, axis=0).reshape(model_width, 3, hidden_share)  40.8 us
  transfers between devices with their start and end apart: 7, of which 6 were waited for; matrix products, arithmetic and copies ran while one was open for 32% of the time, Pallas kernels for 0%

commit v1 on v0

v1 whole, which is shorter than its diff:
```python
import math

import jax
import jax.numpy as jnp
from jax import lax
from jax.sharding import PartitionSpec as P

DH = 128
ROUTE_SCALE = 2.827
EPSILON = 1e-06


def attention(queries, new_keys, new_values, cache_keys, cache_values, cache_lengths):
    steps, rows, features = queries.shape
    heads = features // DH
    cached = cache_keys.shape[1]
    q = queries.reshape(steps, rows, heads, DH)
    keys_old = cache_keys.reshape(rows, cached, heads, DH)
    values_old = cache_values.reshape(rows, cached, heads, DH)
    keys_new = new_keys.reshape(steps, rows, heads, DH)
    values_new = new_values.reshape(steps, rows, heads, DH)
    factor = 1.0 / math.sqrt(DH)
    f32 = jnp.float32
    old = jnp.einsum("trhd,rchd->rhtc", q, keys_old, preferred_element_type=f32) * factor
    in_cache = jnp.arange(cached, dtype=jnp.int32)[None, :] < cache_lengths[:, None]
    old = jnp.where(in_cache[:, None, None, :], old, -1e30)
    new = jnp.einsum("trhd,srhd->rhts", q, keys_new, preferred_element_type=f32) * factor
    order = jnp.arange(steps, dtype=jnp.int32)
    new = jnp.where((order[None, :] <= order[:, None])[None, None], new, -1e30)
    largest = jnp.maximum(jnp.max(old, axis=3, keepdims=True), jnp.max(new, axis=3, keepdims=True))
    old = jnp.exp(old - largest)
    new = jnp.exp(new - largest)
    total = jnp.sum(old, axis=3) + jnp.sum(new, axis=3)
    weighted = jnp.einsum(
        "rhtc,rchd->rhtd", old.astype(jnp.bfloat16), values_old, preferred_element_type=f32
    ) + jnp.einsum(
        "rhts,srhd->rhtd", new.astype(jnp.bfloat16), values_new, preferred_element_type=f32
    )
    out = (weighted / total[..., None]).astype(jnp.bfloat16)
    return out.transpose(0, 2, 1, 3).reshape(rows, steps, features)


def on_device(
    hidden_in,
    queries,
    new_keys,
    new_values,
    cache_keys,
    cache_values,
    cache_lengths,
    expert_ids,
    router_logits,
    norm_gain,
    out_sectioned,
    expert_sectioned,
    bucket_owner,
):
    steps, row_block, width = hidden_in.shape
    n_ep = lax.axis_size("ep")
    n_rep = lax.axis_size("rep")
    me_rep = lax.axis_index("rep")
    me_ep = lax.axis_index("ep")
    half = width // n_rep
    own = steps * row_block
    part = own // n_rep
    f32, bf16 = jnp.float32, jnp.bfloat16
    owners = bucket_owner[0]
    bucket_of = jnp.argsort(owners)

    affinity = jax.nn.sigmoid(router_logits)
    share = ROUTE_SCALE * affinity / jnp.sum(affinity, axis=2, keepdims=True)
    experts = jnp.arange(n_ep, dtype=jnp.int32)
    dense = jnp.sum(jnp.where(expert_ids[..., None] == experts, share[..., None], 0.0), axis=2)
    dense = dense.transpose(1, 0, 2).reshape(own, n_ep)
    mix = lax.all_gather(dense, "ep", axis=0, tiled=False)
    mix = lax.dynamic_index_in_dim(mix, me_ep, axis=2, keepdims=False)
    mix = mix.reshape(n_ep, n_rep, part).transpose(1, 0, 2).reshape(-1, 1)

    heads = attention(queries, new_keys, new_values, cache_keys, cache_values, cache_lengths)
    heads = heads.reshape(n_ep * own, -1)
    partial = jnp.dot(heads, out_sectioned, preferred_element_type=f32).astype(bf16)
    summed = lax.psum_scatter(partial, "ep", scatter_dimension=0, tiled=True)
    swapped = lax.all_to_all(
        summed.reshape(n_rep, part, half), "rep", split_axis=0, concat_axis=0, tiled=True
    )
    attended = swapped.transpose(1, 0, 2).reshape(part, width)
    hidden = hidden_in.transpose(1, 0, 2).reshape(own, width)
    hidden = lax.dynamic_slice_in_dim(hidden, me_rep * part, part, 0)
    residual = hidden.astype(f32) + attended.astype(f32)
    mean_square = jnp.mean(residual * residual, axis=1, keepdims=True)
    normalized = (residual * lax.rsqrt(mean_square + EPSILON) * norm_gain).astype(bf16)

    gathered = lax.all_gather(normalized, "ep", axis=0, tiled=True)
    blocks = gathered.reshape(n_ep * part, n_rep, half).transpose(1, 0, 2)
    blocks = jnp.take(blocks, bucket_of, axis=0)
    arrived = lax.all_to_all(blocks, "rep", split_axis=0, concat_axis=0, tiled=True)
    arrived = arrived.reshape(n_rep * n_ep * part, half)

    weights = expert_sectioned[0]
    gate = jnp.dot(arrived, weights[:, 0], preferred_element_type=f32).astype(bf16)
    up = jnp.dot(arrived, weights[:, 1], preferred_element_type=f32).astype(bf16)
    both = jnp.stack([gate, up])
    both = lax.psum_scatter(both, "rep", scatter_dimension=1, tiled=True).astype(f32)
    activated = (jax.nn.silu(both[0]) * both[1]).astype(bf16)
    activated = lax.all_gather(activated, "rep", axis=0, tiled=True)
    out = jnp.einsum("nf,df->nd", activated, weights[:, 2], preferred_element_type=f32)
    out = (out * mix).astype(bf16)

    back = lax.all_to_all(
        out.reshape(n_rep, n_ep * part, half), "rep", split_axis=0, concat_axis=0, tiled=True
    )
    back = jnp.take(back, owners, axis=0).transpose(1, 0, 2).reshape(n_ep * part, width)
    routed = lax.psum_scatter(back, "ep", scatter_dimension=0, tiled=True)
    layer = (residual + routed.astype(f32)).astype(bf16)
    layer = lax.all_gather(layer, "rep", axis=0, tiled=True)
    return layer.reshape(row_block, steps, width).transpose(1, 0, 2)


def solution(mesh):
    return jax.shard_map(
        on_device,
        mesh=mesh,
        in_specs=(
            P(None, "ep", None),
            P(None, None, "ep"),
            P(None, None, "ep"),
            P(None, None, "ep"),
            P(None, None, "ep"),
            P(None, None, "ep"),
            P(),
            P(None, "ep", None),
            P(None, "ep", None),
            P(),
            P("ep", "rep"),
            P("ep", "rep", None, None),
            P("ep", None),
        ),
        out_specs=P(None, "ep", None),
        check_vma=False,
    )
```

time: 834 us -> 332 us (0.40); the launches traced: 819 us -> 331 us
  waiting for transfers between devices: 481 us -> 185 us
  local copies, waits for them, and re-layouts: 220 us -> 29.1 us
  blocking collectives: 0 us -> 59.5 us
  matrix products: 51.7 us -> 23.9 us
  other arithmetic: 27.1 us -> 11 us
  starting transfers between devices: 24 us -> 8.19 us
    all_to_all x3 -> x2, waiting for transfers between devices: 231 us -> 26.1 us  [the longest x1 22 us: on_device(): lax.all_to_all(out.reshape(n_rep, n_ep * part, half), 'rep', split_axis=0...]
    unnamed x55 -> x19, local copies, waits for them, and re-layouts: 152 us -> 1.17 us
    unnamed x5 -> x4, waiting for transfers between devices: 105 us -> 0.07 us
    reduce_scatter x1 -> x3, waiting for transfers between devices: 49.5 us -> 121 us  [the longest x1 63.4 us: on_device(): summed = lax.psum_scatter(partial, 'ep', scatter_dimension=0, tiled=True)]
    all_gather x2 -> x1, waiting for transfers between devices: 95.8 us -> 38.1 us  [on_device(): gathered = lax.all_gather(normalized, 'ep', axis=0, tiled=True)]
    all_gather x0 -> x3, blocking collectives: none -> 34.3 us  [the longest x1 19.4 us: on_device(): mix = lax.all_gather(dense, 'ep', axis=0, tiled=False)]
    gather x8 -> x2, local copies, waits for them, and re-layouts: 40.8 us -> 6.78 us  [the longest x1 3.39 us: on_device(): jnp.take(back, owners, axis=0).transpose(1, 0, 2)]
    dot_general x23 -> x8, matrix products: 51.7 us -> 23.9 us  [the longest x1 6.47 us: on_device(): jnp.einsum('nf,df->nd', activated, weights[:, 2], preferred_element_type=...]
  transfers between devices with their start and end apart: 7 -> 6, of which waited for: 6 -> 5; matrix products, arithmetic and copies ran while one was open for 32% -> 0% of each run, Pallas kernels for 0% -> 0%
where the time goes in v1:
time: 332 us; the launch traced here: 331 us
  waiting for transfers between devices  185 us (56%)
  blocking collectives  59.5 us (18%)
  local copies, waits for them, and re-layouts  29.1 us (9%)
  matrix products  23.9 us (7%)
  between operations  13.5 us (4%)
  other arithmetic  11 us (3%)
  starting transfers between devices  8.19 us (2%)
    reduce_scatter x1, waiting for transfers between devices, on_device(): summed = lax.psum_scatter(partial, 'ep', scatter_dimension=0, tiled=True)  63.4 us
    reduce_scatter x1, waiting for transfers between devices, on_device(): routed = lax.psum_scatter(back, 'ep', scatter_dimension=0, tiled=True)  57.6 us
    all_gather x1, waiting for transfers between devices, on_device(): gathered = lax.all_gather(normalized, 'ep', axis=0, tiled=True)  38.1 us
    all_to_all x1, blocking collectives, on_device(): lax.all_to_all(blocks, 'rep', split_axis=0, concat_axis=0, tiled=True)  25.2 us
    all_to_all x1, waiting for transfers between devices, on_device(): lax.all_to_all(out.reshape(n_rep, n_ep * part, half), 'rep', split_axis=0...  22 us
    all_gather x1, blocking collectives, on_device(): mix = lax.all_gather(dense, 'ep', axis=0, tiled=False)  19.4 us
    all_gather x1, blocking collectives, on_device(): activated = lax.all_gather(activated, 'rep', axis=0, tiled=True)  9.41 us
  transfers between devices with their start and end apart: 6, of which 5 were waited for; matrix products, arithmetic and copies ran while one was open for 0% of the time, Pallas kernels for 0%

profile of v1, /device:TPU:0, one launch (start us, length us, event | category | flops | bytes accessed | tf_op | source)
XLA Modules:
  0.0 330.5 jit_solution(3577825658927616849)
XLA Ops:
  6.5 1.2 reshape.103
  7.7 1.1 reshape.105
  10.0 3.0 fusion.52
  14.4 1.0 reshape.107
  16.0 1.0 fusion.30
  17.0 0.9 copy-done.1
  18.0 2.4 convolution_convert_fusion
  20.4 63.4 %reduce-scatter.4.cloned.1.call-done = bf16[16,3584]{1,0:T(8,128)(2,1)} async-done(((bf16[256,3584]{1,0:T(8,128)(2,1)}), bf16[16,3584]{1,0:T(8,128)(2,1)}) %reduce-scatter.4.cloned.1.call-update) | async-done | bytes 114704 | tf_op jit(solution)/shard_map/reduce_scatter | solution.py:82
  83.8 3.4 %all-to-all-start = ((bf16[2,8,3584]{2,1,0:T(8,128)(2,1)}), bf16[2,8,3584]{2,1,0:T(8,128)(2,1)S(1)}, u32[]{:S(2)}, u32[]{:S(2)}) async-start(bf16[2,8,3584]{2,1,0:T(8,128)(2,1)} %bitcast.116), calls=%async_computation.1 | async-start | bytes 229376 | tf_op jit(solution)/shard_map/all_to_all | solution.py:83
  87.4 4.1 %all-to-all-done = bf16[2,8,3584]{2,1,0:T(8,128)(2,1)S(1)} async-done(((bf16[2,8,3584]{2,1,0:T(8,128)(2,1)}), bf16[2,8,3584]{2,1,0:T(8,128)(2,1)S(1)}, u32[]{:S(2)}, u32[]{:S(2)}) %all-to-all-start) | async-done | bytes 114720 | tf_op jit(solution)/shard_map/all_to_all | solution.py:83
  93.2 38.1 %all-gather.2.cloned.1.call-done = bf16[128,7168]{1,0:T(8,128)(2,1)} async-done(((bf16[8,7168]{1,0:T(8,128)(2,1)}), bf16[128,7168]{1,0:T(8,128)(2,1)}) %all-gather.2.cloned.1.call-update) | async-done | bytes 1835024 | tf_op jit(solution)/shard_map/all_gather | solution.py:93
  131.3 3.9 %copy.135 = bf16[128,7168]{0,1:T(8,128)(2,1)} copy(bf16[128,7168]{1,0:T(8,128)(2,1)} %all-gather.2.cloned.1.call-done) | data formatting | bytes 3670016 | tf_op jit(solution)/shard_map/all_gather | solution.py:93
  135.2 3.9 %copy.136 = bf16[128,2,3584]{2,0,1:T(8,128)(2,1)} copy(bf16[128,2,3584]{0,2,1:T(8,128)(2,1)} %bitcast.104) | data formatting | bytes 3670016 | tf_op jit(solution)/shard_map/reshape | solution.py:94
  139.1 3.4 %gather_fusion = bf16[2,128,3584]{2,1,0:T(8,128)(2,1)} fusion(bf16[2,128,3584]{2,1,0:T(8,128)(2,1)} %bitcast.106, s32[1024]{0:T(1024)S(1)} %pad_clamp_fusion.1), kind=kCustom, calls=%fused_computation.clone | custom fusion | bytes 3670024 | tf_op jit(solution)/shard_map/jit(_take)/gather | solution.py:95
  142.4 1.7 broadcast_select_fusion
  144.2 25.2 %all_to_all.15 = bf16[2,128,3584]{2,1,0:T(8,128)(2,1)S(1)} all-to-all(bf16[2,128,3584]{2,1,0:T(8,128)(2,1)S(1)} %broadcast_select_fusion), channel_id=1, replica_groups=mesh['rep'=2,'ep'=16] {'rep'}, dimensions={0} | all-to-all | bytes 3670016 | tf_op jit(solution)/shard_map/all_to_all | solution.py:96
  169.4 5.1 %fusion.13 = bf16[1,256,1024]{2,1,0:T(8,128)(2,1)S(1)} fusion(bf16[256,3584]{1,0:T(8,128)(2,1)S(1)} %bitcast.111, bf16[3584,3,1024]{2,0,1:T(8,128)(2,1)} %bitcast.120), kind=kOutput, calls=%fused_computation.21 | convolution fusion | flops 1879310336 | bytes 9699328 | tf_op jit(solution)/shard_map/dot_general | solution.py:101
  174.6 5.1 %fusion.14 = bf16[1,256,1024]{2,1,0:T(8,128)(2,1)S(1)} fusion(bf16[256,3584]{1,0:T(8,128)(2,1)S(1)} %bitcast.112, bf16[3584,3,1024]{2,0,1:T(8,128)(2,1)} %bitcast.121), kind=kOutput, calls=%fused_computation.22 | convolution fusion | flops 1879310336 | bytes 9699328 | tf_op jit(solution)/shard_map/dot_general | solution.py:100
  179.7 1.1 pad_maximum_fusion
  181.1 19.4 %all_gather.14 = f32[16,16,16]{2,1,0:T(8,128)S(1)} all-gather(f32[1,16,16]{2,1,0:T(8,128)S(1)} %bitcast.118), channel_id=1, replica_groups=mesh['rep'=2,'ep'=16] {'ep'}, dimensions={0}, use_global_device_ids=true | all-gather | bytes 17408 | tf_op jit(solution)/shard_map/all_gather | solution.py:75
  201.0 1.1 convert_element_type.60
  202.3 9.4 %all_gather.13 = bf16[256,1024]{1,0:T(8,128)(2,1)S(1)} all-gather(bf16[128,1024]{1,0:T(8,128)(2,1)S(1)} %fusion.34), channel_id=1, replica_groups=mesh['rep'=2,'ep'=16] {'rep'}, dimensions={0}, use_global_device_ids=true | all-gather | bytes 786432 | tf_op jit(solution)/shard_map/all_gather | solution.py:105
  211.7 6.5 %fusion.4 = bf16[256,3584]{1,0:T(8,128)(2,1)} fusion(bf16[256,1024]{1,0:T(8,128)(2,1)S(1)} %all_gather.13, bf16[3584,3,1024]{2,0,1:T(8,128)(2,1)} %bitcast.122, f32[256]{0:T(256)S(1)} %mul.71), kind=kOutput, calls=%fused_computation.10 | convolution fusion | flops 1880883200 | bytes 9700352 | tf_op jit(solution)/shard_map/nf,df->nd/dot_general | solution.py:106
  218.2 4.7 %all-to-all-start.2 = ((bf16[2,128,3584]{2,1,0:T(8,128)(2,1)}), bf16[2,128,3584]{2,1,0:T(8,128)(2,1)}, u32[]{:S(2)}, u32[]{:S(2)}) async-start(bf16[2,128,3584]{2,1,0:T(8,128)(2,1)} %bitcast.110), calls=%async_computation.4 | async-start | bytes 3670016 | tf_op jit(solution)/shard_map/all_to_all | solution.py:109
  223.0 22.0 %all-to-all-done.2 = bf16[2,128,3584]{2,1,0:T(8,128)(2,1)} async-done(((bf16[2,128,3584]{2,1,0:T(8,128)(2,1)}), bf16[2,128,3584]{2,1,0:T(8,128)(2,1)}, u32[]{:S(2)}, u32[]{:S(2)}) %all-to-all-start.2) | async-done | bytes 1835040 | tf_op jit(solution)/shard_map/all_to_all | solution.py:109
  245.0 3.4 %gather_fusion.1 = bf16[2,128,3584]{2,1,0:T(8,128)(2,1)} fusion(bf16[2,128,3584]{2,1,0:T(8,128)(2,1)} %all-to-all-done.2, s32[1024]{0:T(1024)S(1)} %pad_clamp_fusion), kind=kCustom, calls=%fused_computation.1.clone | custom fusion | bytes 3670024 | tf_op jit(solution)/shard_map/jit(_take)/gather | solution.py:112
  248.4 3.0 select_bitcast_fusion
  251.3 3.8 %copy.140 = bf16[128,2,3584]{0,2,1:T(8,128)(2,1)} copy(bf16[128,2,3584]{2,0,1:T(8,128)(2,1)} %select_bitcast_fusion) | data formatting | bytes 3670016 | tf_op jit(solution)/shard_map/transpose | solution.py:112
  255.1 3.9 %copy.141 = bf16[128,7168]{1,0:T(8,128)(2,1)} copy(bf16[128,7168]{0,1:T(8,128)(2,1)} %bitcast.105) | data formatting | bytes 3670016 | tf_op jit(solution)/shard_map/reshape | solution.py:112
  259.1 57.6 %reduce-scatter.8.cloned.1.call-done = bf16[8,7168]{1,0:T(8,128)(2,1)} async-done(((bf16[128,7168]{1,0:T(8,128)(2,1)}), bf16[8,7168]{1,0:T(8,128)(2,1)}) %reduce-scatter.8.cloned.1.call-update) | async-done | bytes 114704 | tf_op jit(solution)/shard_map/reduce_scatter | solution.py:113
  316.7 0.9 add_convert_fusion
  317.6 5.5 %all_gather.15 = bf16[16,7168]{1,0:T(8,128)(2,1)S(1)} all-gather(bf16[8,7168]{1,0:T(8,128)(2,1)S(1)} %add_convert_fusion), channel_id=1, replica_groups=mesh['rep'=2,'ep'=16] {'rep'}, dimensions={0}, use_global_device_ids=true | all-gather | bytes 344064 | tf_op jit(solution)/shard_map/all_gather | solution.py:115
  (65 shorter events, 6.8 us)
Async XLA Ops:
  6.5 9.4 %copy-start = (bf16[64,32,512]{2,1,0:T(8,128)(2,1)S(1)}, bf16[64,32,512]{2,1,0:T(8,128)(2,1)}, u32[]{:S(2)}) copy-start(bf16[64,32,512]{2,1,0:T(8,128)(2,1)} %param.20) | copy-start | bytes 6291460
  6.5 3.4 %copy-start.6 = (s32[64]{0:T(128)S(1)}, s32[64]{0:T(128)}, u32[]{:S(2)}) copy-start(s32[64]{0:T(128)} %param.21) | copy-start | bytes 772
  6.5 77.2 %reduce-scatter.4.cloned.1.call-start = ((), (), s32[]{:S(2)}) async-start(), calls=%async_computation.6 | async-start | bytes 1949696 | tf_op jit(solution)/shard_map/reduce_scatter | solution.py:82
  7.7 1.1 copy-start.2
  15.9 2.0 copy-start.1
  20.4 66.8 %copy-start.3 = (bf16[4,4,7168]{2,1,0:T(4,128)(2,1)S(1)}, bf16[4,4,7168]{2,1,0:T(4,128)(2,1)}, u32[]{:S(2)}) copy-start(bf16[4,4,7168]{2,1,0:T(4,128)(2,1)} %param.15) | copy-start | bytes 688132
  20.4 71.3 %copy-start.4 = (f32[7168]{0:T(1024)S(1)}, f32[7168]{0:T(1024)}, u32[]{:S(2)}) copy-start(f32[7168]{0:T(1024)} %param.24) | copy-start | bytes 86020
  20.4 72.2 %copy-start.8 = (s32[1,2]{1,0:T(1,128)S(1)}, s32[1,2]{1,0:T(1,128)}, u32[]{:S(2)}) copy-start(s32[1,2]{1,0:T(1,128)} %param.27) | copy-start | bytes 28
  83.8 7.7 %all-to-all-start = ((bf16[2,8,3584]{2,1,0:T(8,128)(2,1)}), bf16[2,8,3584]{2,1,0:T(8,128)(2,1)S(1)}, u32[]{:S(2)}, u32[]{:S(2)}) async-start(bf16[2,8,3584]{2,1,0:T(8,128)(2,1)} %bitcast.116), calls=%async_computation.1 | async-start | bytes 229376 | tf_op jit(solution)/shard_map/all_to_all | solution.py:83
  87.1 44.2 %all-gather.2.cloned.1.call-start = ((), (), s32[]{:S(2)}) async-start(), calls=%async_computation.7 | async-start | bytes 1949696 | tf_op jit(solution)/shard_map/all_gather | solution.py:93
  92.5 108.5 %reduce-scatter.6.cloned.1.call-start = ((), (), s32[]{:S(2)}) async-start(), calls=%async_computation.8 | async-start | bytes 1572864 | tf_op jit(solution)/shard_map/reduce_scatter | solution.py:103
  179.7 1.1 copy-start.7
  179.7 1.2 copy-start.5
  218.2 26.8 %all-to-all-start.2 = ((bf16[2,128,3584]{2,1,0:T(8,128)(2,1)}), bf16[2,128,3584]{2,1,0:T(8,128)(2,1)}, u32[]{:S(2)}, u32[]{:S(2)}) async-start(bf16[2,128,3584]{2,1,0:T(8,128)(2,1)} %bitcast.110), calls=%async_computation.4 | async-start | bytes 3670016 | tf_op jit(solution)/shard_map/all_to_all | solution.py:109
  222.9 93.8 %reduce-scatter.8.cloned.1.call-start = ((), (), s32[]{:S(2)}) async-start(), calls=%async_computation.9 | async-start | bytes 1949696 | tf_op jit(solution)/shard_map/reduce_scatter | solution.py:113
Sparse Core Ops, SparseCore 0:
  20.5 63.1 reduce-scatter.3
  92.6 38.6 all-gather.1
  181.0 18.0 reduce-scatter.5
  259.2 57.4 reduce-scatter.7

commit v2 on v1

--- a/solution.py
+++ b/solution.py
@@ -1,13 +1,18 @@
+import functools
 import math
 
 import jax
 import jax.numpy as jnp
 from jax import lax
+from jax.experimental import pallas as pl
+from jax.experimental.pallas import tpu as pltpu
 from jax.sharding import PartitionSpec as P
 
 DH = 128
 ROUTE_SCALE = 2.827
 EPSILON = 1e-06
+MESH = pl.DeviceIdType.MESH
+VMEM_BYTES = 48 * 1024 * 1024
 
 
 def attention(queries, new_keys, new_values, cache_keys, cache_values, cache_lengths):
@@ -38,6 +43,349 @@
     )
     out = (weighted / total[..., None]).astype(jnp.bfloat16)
     return out.transpose(0, 2, 1, 3).reshape(rows, steps, features)
+
+
+def place(n_ep):
+    rep = lax.axis_index("rep")
+    ep = lax.axis_index("ep")
+    return rep, ep // 4, (ep // 2) % 2, ep % 2
+
+
+def neighbours(n_far, rep, far, near, core):
+    def at(rep_, far_, near_, core_):
+        return (rep_, far_ * 4 + near_ * 2 + core_)
+
+    others = [lax.rem(far + d, n_far) for d in range(1, n_far)]
+    return (
+        at(1 - rep, far, near, core),
+        at(rep, far, near, 1 - core),
+        at(rep, far, 1 - near, core),
+        others,
+        [at(rep, other, near, core) for other in others],
+    )
+
+
+def greet(devices):
+    barrier = pltpu.get_barrier_semaphore()
+    for device in devices:
+        pl.semaphore_signal(barrier, inc=1, device_id=device, device_id_type=MESH)
+    pl.semaphore_wait(barrier, len(devices))
+
+
+def send(src, dst, sems, index, device):
+    copy = pltpu.make_async_remote_copy(
+        src_ref=src,
+        dst_ref=dst,
+        send_sem=sems.at[(0,) + index],
+        recv_sem=sems.at[(1,) + index],
+        device_id=device,
+        device_id_type=MESH,
+    )
+    copy.start()
+    return copy
+
+
+def add_rows(x, y):
+    return (x.astype(jnp.float32) + y.astype(jnp.float32)).astype(jnp.bfloat16)
+
+
+class Scatter:
+    def __init__(self, spot, links, source, from_core, half, from_near, quarter, from_far, sems):
+        _, self.far, self.near, self.core = spot
+        _, self.to_core, self.to_near, self.others, self.to_far = links
+        self.source, self.from_core, self.half = source, from_core, half
+        self.from_near, self.quarter, self.from_far = from_near, quarter, from_far
+        self.sems = sems
+        self.n_far = quarter.shape[1]
+
+    def first(self, k):
+        return send(
+            self.source.at[k, :, 1 - self.core], self.from_core.at[k], self.sems, (k, 0),
+            self.to_core,
+        )
+
+    def second(self, k):
+        def add(j, _):
+            self.half[k, j // 2, j % 2] = add_rows(
+                self.source[k, j, self.core], self.from_core[k, j]
+            )
+            return 0
+
+        lax.fori_loop(0, 2 * self.n_far, add, 0)
+        return send(
+            self.half.at[k, :, 1 - self.near], self.from_near.at[k], self.sems, (k, 1),
+            self.to_near,
+        )
+
+    def third(self, k):
+        def add(j, _):
+            self.quarter[k, j] = add_rows(self.half[k, j, self.near], self.from_near[k, j])
+            return 0
+
+        lax.fori_loop(0, self.n_far, add, 0)
+        return [
+            send(self.quarter.at[k, other], self.from_far.at[k, d], self.sems, (k, 2 + d), device)
+            for d, (other, device) in enumerate(zip(self.others, self.to_far))
+        ]
+
+    def total(self, k):
+        total = self.quarter[k, self.far].astype(jnp.float32)
+        for d in range(self.n_far - 1):
+            total += self.from_far[k, d].astype(jnp.float32)
+        return total
+
+
+def scatter_scratch(n_far, chunks, block):
+    bf16 = jnp.bfloat16
+    return [
+        pltpu.VMEM((chunks, 2 * n_far, 2) + block, bf16),
+        pltpu.VMEM((chunks, 2 * n_far) + block, bf16),
+        pltpu.VMEM((chunks, n_far, 2) + block, bf16),
+        pltpu.VMEM((chunks, n_far) + block, bf16),
+        pltpu.VMEM((chunks, n_far) + block, bf16),
+        pltpu.VMEM((chunks, n_far - 1) + block, bf16),
+        pltpu.SemaphoreType.DMA((2, chunks, n_far + 1)),
+    ]
+
+
+def dispatch_kernel(
+    n_far,
+    flag_ref,
+    heads_ref,
+    proj_ref,
+    hidden_ref,
+    gain_ref,
+    rows_ref,
+    residual_ref,
+    source,
+    from_core,
+    half,
+    from_near,
+    quarter,
+    from_far,
+    sems,
+    attended,
+    gathered,
+    staged,
+    swap_sems,
+    ring_sems,
+    cross_sems,
+):
+    f32, bf16 = jnp.float32, jnp.bfloat16
+    spot = rep, far, near, core = place(4 * n_far)
+    links = to_rep, to_core, to_near, others, to_far = neighbours(n_far, *spot)
+    greet([to_rep, to_core, to_near] + to_far)
+    scatter = Scatter(
+        spot, links, source, from_core, half, from_near, quarter, from_far, sems
+    )
+    own, piece = attended.shape[2], attended.shape[3]
+    width = 4 * piece
+
+    first = []
+    for k in range(2):
+        product = jnp.dot(
+            heads_ref[...], proj_ref[:, k * piece : (k + 1) * piece], preferred_element_type=f32
+        )
+        source[k] = product.astype(bf16).reshape(2 * n_far, 2, own, piece)
+        first.append(scatter.first(k))
+    second = []
+    for k in range(2):
+        first[k].wait()
+        second.append(scatter.second(k))
+    third = []
+    for k in range(2):
+        second[k].wait()
+        third.append(scatter.third(k))
+    swaps = []
+    for k in range(2):
+        for copy in third[k]:
+            copy.wait()
+        attended[rep, k] = scatter.total(k).astype(bf16)
+        swaps.append(
+            send(attended.at[rep, k], attended.at[rep, k], swap_sems, (k,), to_rep)
+        )
+    for copy in swaps:
+        copy.wait()
+
+    squares = jnp.zeros((own, 1), f32)
+    for h in range(2):
+        for k in range(2):
+            start = (2 * h + k) * piece
+            residual = hidden_ref[:, start : start + piece].astype(f32)
+            residual += attended[h, k].astype(f32)
+            squares += jnp.sum(residual * residual, axis=1, keepdims=True)
+    scale = lax.rsqrt(squares / width + EPSILON)
+    for h in range(2):
+        lanes = pl.ds(pl.multiple_of((2 * h + rep) * piece, 128), piece)
+        residual = hidden_ref[:, lanes].astype(f32) + attended[h, rep].astype(f32)
+        residual_ref[h] = residual
+        gathered[far, near, core, h] = (residual * scale * gain_ref[:, lanes]).astype(bf16)
+
+    flag = flag_ref[0, 0]
+    mine = pl.ds(pl.multiple_of(rep * piece, 128), piece)
+    pending = []
+
+    def cross(f, n, c, index):
+        low, high = gathered[f, n, c, 0], gathered[f, n, c, 1]
+        rows_ref[f, n, c, :, mine] = jnp.where(flag == 0, low, high)
+        staged[f, n, c] = jnp.where(flag == 0, high, low)
+        pending.append(
+            send(staged.at[f, n, c], rows_ref.at[f, n, c, :, mine], cross_sems, (index,), to_rep)
+        )
+
+    def pass_on(f, n, c, index, device):
+        block = gathered.at[f, n, c]
+        return send(block, block, ring_sems, (index,), device)
+
+    far_copies = [
+        pass_on(far, near, core, d, device) for d, device in enumerate(to_far)
+    ]
+    base = n_far - 1
+    for d in range(n_far):
+        behind = lax.rem(far + n_far - d, n_far)
+        if d > 0:
+            far_copies[d - 1].wait_recv()
+        near_copy = pass_on(behind, near, core, base + 3 * d, to_near)
+        core_copy = pass_on(behind, near, core, base + 3 * d + 1, to_core)
+        cross(behind, near, core, 4 * d)
+        near_copy.wait_recv()
+        other_copy = pass_on(behind, 1 - near, core, base + 3 * d + 2, to_core)
+        cross(behind, 1 - near, core, 4 * d + 1)
+        core_copy.wait_recv()
+        cross(behind, near, 1 - core, 4 * d + 2)
+        other_copy.wait_recv()
+        cross(behind, 1 - near, 1 - core, 4 * d + 3)
+        near_copy.wait_send()
+        core_copy.wait_send()
+        other_copy.wait_send()
+    for copy in far_copies:
+        copy.wait_send()
+    for copy in pending:
+        copy.wait()
+
+
+def dispatch(n_ep, flag, heads, projection, hidden, gain):
+    n_far = n_ep // 4
+    own, width = hidden.shape
+    piece = width // 4
+    bf16 = jnp.bfloat16
+    vmem = pl.BlockSpec(memory_space=pltpu.VMEM)
+    return pl.pallas_call(
+        functools.partial(dispatch_kernel, n_far),
+        out_shape=(
+            jax.ShapeDtypeStruct((n_far, 2, 2, own, 2 * piece), bf16),
+            jax.ShapeDtypeStruct((2, own, piece), jnp.float32),
+        ),
+        in_specs=[pl.BlockSpec(memory_space=pltpu.SMEM)] + [vmem] * 4,
+        out_specs=(vmem, vmem),
+        scratch_shapes=scatter_scratch(n_far, 2, (own, piece))
+        + [
+            pltpu.VMEM((2, 2, own, piece), bf16),
+            pltpu.VMEM((n_far, 2, 2, 2, own, piece), bf16),
+            pltpu.VMEM((n_far, 2, 2, own, piece), bf16),
+            pltpu.SemaphoreType.DMA((2, 2)),
+            pltpu.SemaphoreType.DMA((2, 4 * n_far - 1)),
+            pltpu.SemaphoreType.DMA((2, 4 * n_far)),
+        ],
+        compiler_params=pltpu.CompilerParams(
+            collective_id=0, has_side_effects=True, vmem_limit_bytes=VMEM_BYTES
+        ),
+    )(flag, heads, projection, hidden, gain)
+
+
+def combine_kernel(
+    n_far,
+    flag_ref,
+    out_ref,
+    residual_ref,
+    layer_ref,
+    source,
+    from_core,
+    half,
+    from_near,
+    quarter,
+    from_far,
+    sems,
+    from_rep,
+    cross_sems,
+    last_sems,
+):
+    spot = rep, far, near, core = place(4 * n_far)
+    links = to_rep, to_core, to_near, others, to_far = neighbours(n_far, *spot)
+    greet([to_rep, to_core, to_near] + to_far)
+    scatter = Scatter(
+        spot, links, source, from_core, half, from_near, quarter, from_far, sems
+    )
+    piece = residual_ref.shape[2]
+    chunk = piece // 2
+    flag = flag_ref[0, 0]
+
+    def lanes(owner, k):
+        return pl.ds(pl.multiple_of(owner * piece + k * chunk, 128), chunk)
+
+    crossing = [
+        send(out_ref.at[:, :, :, lanes(1 - rep, k)], from_rep.at[k], cross_sems, (k,), to_rep)
+        for k in range(2)
+    ]
+    first = []
+    for k in range(2):
+        crossing[k].wait()
+
+        def arrange(j, _):
+            mine = out_ref[j // 2, j % 2, :, lanes(rep, k)]
+            other = from_rep[k, j // 2, j % 2]
+            source[k, j // 2, j % 2, 0] = jnp.where(flag == 0, mine, other)
+            source[k, j // 2, j % 2, 1] = jnp.where(flag == 0, other, mine)
+            return 0
+
+        lax.fori_loop(0, 4 * n_far, arrange, 0)
+        first.append(scatter.first(k))
+        if k == 0:
+            first[0].wait()
+            second = [scatter.second(0)]
+    second[0].wait()
+    third = [scatter.third(0)]
+    first[1].wait()
+    second.append(scatter.second(1))
+    second[1].wait()
+    third.append(scatter.third(1))
+    last = []
+    for k in range(2):
+        for copy in third[k]:
+            copy.wait()
+        layer = residual_ref[:, :, k * chunk : (k + 1) * chunk] + scatter.total(k)
+        layer = layer.astype(jnp.bfloat16)
+        for h in range(2):
+            spot_lanes = pl.ds(
+                pl.multiple_of((2 * h + rep) * piece + k * chunk, 128), chunk
+            )
+            layer_ref[:, spot_lanes] = layer[h]
+            block = layer_ref.at[:, spot_lanes]
+            last.append(send(block, block, last_sems, (2 * k + h,), to_rep))
+    for copy in last:
+        copy.wait()
+
+
+def combine(n_ep, flag, out, residual):
+    n_far = n_ep // 4
+    _, own, piece = residual.shape
+    bf16 = jnp.bfloat16
+    vmem = pl.BlockSpec(memory_space=pltpu.VMEM)
+    return pl.pallas_call(
+        functools.partial(combine_kernel, n_far),
+        out_shape=jax.ShapeDtypeStruct((own, 4 * piece), bf16),
+        in_specs=[pl.BlockSpec(memory_space=pltpu.SMEM)] + [vmem] * 2,
+        out_specs=vmem,
+        scratch_shapes=scatter_scratch(n_far, 2, (2, own, piece // 2))
+        + [
+            pltpu.VMEM((2, 2 * n_far, 2, own, piece // 2), bf16),
+            pltpu.SemaphoreType.DMA((2, 2)),
+            pltpu.SemaphoreType.DMA((2, 4)),
+        ],
+        compiler_params=pltpu.CompilerParams(
+            collective_id=1, has_side_effects=True, vmem_limit_bytes=VMEM_BYTES
+        ),
+    )(flag, out.reshape(2 * n_far, 2, own, 2 * piece), residual)
 
 
 def on_device(
@@ -74,27 +422,35 @@
     dense = dense.transpose(1, 0, 2).reshape(own, n_ep)
     mix = lax.all_gather(dense, "ep", axis=0, tiled=False)
     mix = lax.dynamic_index_in_dim(mix, me_ep, axis=2, keepdims=False)
-    mix = mix.reshape(n_ep, n_rep, part).transpose(1, 0, 2).reshape(-1, 1)
 
     heads = attention(queries, new_keys, new_values, cache_keys, cache_values, cache_lengths)
     heads = heads.reshape(n_ep * own, -1)
-    partial = jnp.dot(heads, out_sectioned, preferred_element_type=f32).astype(bf16)
-    summed = lax.psum_scatter(partial, "ep", scatter_dimension=0, tiled=True)
-    swapped = lax.all_to_all(
-        summed.reshape(n_rep, part, half), "rep", split_axis=0, concat_axis=0, tiled=True
-    )
-    attended = swapped.transpose(1, 0, 2).reshape(part, width)
     hidden = hidden_in.transpose(1, 0, 2).reshape(own, width)
-    hidden = lax.dynamic_slice_in_dim(hidden, me_rep * part, part, 0)
-    residual = hidden.astype(f32) + attended.astype(f32)
-    mean_square = jnp.mean(residual * residual, axis=1, keepdims=True)
-    normalized = (residual * lax.rsqrt(mean_square + EPSILON) * norm_gain).astype(bf16)
-
-    gathered = lax.all_gather(normalized, "ep", axis=0, tiled=True)
-    blocks = gathered.reshape(n_ep * part, n_rep, half).transpose(1, 0, 2)
-    blocks = jnp.take(blocks, bucket_of, axis=0)
-    arrived = lax.all_to_all(blocks, "rep", split_axis=0, concat_axis=0, tiled=True)
-    arrived = arrived.reshape(n_rep * n_ep * part, half)
+    by_kernel = n_rep == 2 and n_ep % 4 == 0 and own % 16 == 0 and half % 512 == 0
+    if by_kernel:
+        flag = (owners[0] != me_rep).astype(jnp.int32).reshape(1, 1)
+        arrived, residual = dispatch(n_ep, flag, heads, out_sectioned, hidden, norm_gain[None])
+        arrived = arrived.reshape(n_ep * own, half)
+    else:
+        partial = jnp.dot(heads, out_sectioned, preferred_element_type=f32).astype(bf16)
+        summed = lax.psum_scatter(partial, "ep", scatter_dimension=0, tiled=True)
+        swapped = lax.all_to_all(
+            summed.reshape(n_rep, part, half), "rep", split_axis=0, concat_axis=0, tiled=True
+        )
+        attended = swapped.transpose(1, 0, 2).reshape(part, width)
+        hidden = lax.dynamic_slice_in_dim(hidden, me_rep * part, part, 0)
+        residual = hidden.astype(f32) + attended.astype(f32)
+        mean_square = jnp.mean(residual * residual, axis=1, keepdims=True)
+        normalized = (residual * lax.rsqrt(mean_square + EPSILON) * norm_gain).astype(bf16)
+
+        gathered = lax.all_gather(normalized, "ep", axis=0, tiled=True)
+        blocks = gathered.reshape(n_ep * part, n_rep, half).transpose(1, 0, 2)
+        blocks = jnp.take(blocks, bucket_of, axis=0)
+        arrived = lax.all_to_all(blocks, "rep", split_axis=0, concat_axis=0, tiled=True)
+        arrived = arrived.reshape(n_rep * n_ep * part, half)
+
+        mix = mix.reshape(n_ep, n_rep, part).transpose(1, 0, 2)
+    mix = mix.reshape(-1, 1)
 
     weights = expert_sectioned[0]
     gate = jnp.dot(arrived, weights[:, 0], preferred_element_type=f32).astype(bf16)
@@ -106,6 +462,9 @@
     out = jnp.einsum("nf,df->nd", activated, weights[:, 2], preferred_element_type=f32)
     out = (out * mix).astype(bf16)
 
+    if by_kernel:
+        layer = combine(n_ep, flag, out, residual)
+        return layer.reshape(row_block, steps, width).transpose(1, 0, 2)
     back = lax.all_to_all(
         out.reshape(n_rep, n_ep * part, half), "rep", split_axis=0, concat_axis=0, tiled=True
     )

time: 332 us -> 176 us (0.53)
  waiting for transfers between devices: 185 us -> 1.58 us
  Pallas kernels: 0 us -> 101 us
  blocking collectives: 59.5 us -> 29.3 us
  local copies, waits for them, and re-layouts: 29.1 us -> 5.81 us
  starting transfers between devices: 8.19 us -> 0.01 us
  other arithmetic: 11 us -> 3.72 us
  matrix products: 23.9 us -> 20.3 us
    reduce_scatter x2 -> x0, waiting for transfers between devices: 121 us -> none  [the longest x1 63.4 us: on_device(): summed = lax.psum_scatter(partial, 'ep', scatter_dimension=0, tiled=True)]
    pallas_call x0 -> x2, Pallas kernels: none -> 101 us  [the longest x1 58.3 us: dispatch(): pl.pallas_call(functools.partial(dispatch_kernel, n_far), out_shape=(jax....]
    all_gather x1 -> x0, waiting for transfers between devices: 38.1 us -> none  [on_device(): gathered = lax.all_gather(normalized, 'ep', axis=0, tiled=True)]
    all_to_all x2 -> x0, waiting for transfers between devices: 26.1 us -> none  [the longest x1 22 us: on_device(): lax.all_to_all(out.reshape(n_rep, n_ep * part, half), 'rep', split_axis=0...]
    all_to_all x1 -> x0, blocking collectives: 25.2 us -> none  [on_device(): lax.all_to_all(blocks, 'rep', split_axis=0, concat_axis=0, tiled=True)]
    all_to_all x2 -> x0, starting transfers between devices: 8.06 us -> none  [the longest x1 4.7 us: on_device(): lax.all_to_all(out.reshape(n_rep, n_ep * part, half), 'rep', split_axis=0...]
    reshape x2 -> x0, local copies, waits for them, and re-layouts: 7.79 us -> none  [the longest x1 3.94 us: on_device(): jnp.take(back, owners, axis=0).transpose(1, 0, 2)]
    gather x2 -> x0, local copies, waits for them, and re-layouts: 6.78 us -> none  [the longest x1 3.39 us: on_device(): jnp.take(back, owners, axis=0).transpose(1, 0, 2)]
  transfers between devices with their start and end apart: 6 -> 1, of which waited for: 5 -> 1; matrix products, arithmetic and copies ran while one was open for 0% -> 0% of each run, Pallas kernels for 0% -> 0%
where the time goes in v2:
time: 176 us; the launch traced here: 175 us
  Pallas kernels  101 us (57%)
  blocking collectives  29.3 us (17%)
  matrix products  20.3 us (12%)
  between operations  13.7 us (8%)
  local copies, waits for them, and re-layouts  5.81 us (3%)
  other arithmetic  3.72 us (2%)
    pallas_call x1, Pallas kernels, dispatch(): pl.pallas_call(functools.partial(dispatch_kernel, n_far), out_shape=(jax....  58.3 us
    pallas_call x1, Pallas kernels, combine(): pl.pallas_call(functools.partial(combine_kernel, n_far), out_shape=jax.Sh...  42.4 us
    all_gather x1, blocking collectives, on_device(): mix = lax.all_gather(dense, 'ep', axis=0, tiled=False)  20.4 us
    all_gather x1, blocking collectives, on_device(): activated = lax.all_gather(activated, 'rep', axis=0, tiled=True)  8.89 us
    dot_general x1, matrix products, on_device(): jnp.einsum('nf,df->nd', activated, weights[:, 2], preferred_element_type=...  5.18 us
    dot_general x1, matrix products, on_device(): jnp.dot(arrived, weights[:, 1], preferred_element_type=f32).astype(bf16)  5.14 us
    dot_general x1, matrix products, on_device(): jnp.dot(arrived, weights[:, 0], preferred_element_type=f32).astype(bf16)  5.14 us
  transfers between devices with their start and end apart: 1, of which 1 were waited for; matrix products, arithmetic and copies ran while one was open for 0% of the time, Pallas kernels for 0%

profile of v2, /device:TPU:0, one launch (start us, length us, event | category | flops | bytes accessed | tf_op | source)
XLA Modules:
  0.0 175.2 jit_solution(17809784593077682501)
XLA Ops:
  6.6 1.2 reshape.82
  7.7 1.1 reshape.84
  8.9 0.4 fusion.40
  9.3 0.3 copy.86
  9.6 0.1 fusion.45
  9.8 0.1 copy.87
  10.0 3.0 %fusion.50 = (f32[64,4,4]{2,1,0:T(4,128)S(1)}, f32[64,4,4,32]{3,2,1,0:T(4,128)S(1)}) fusion(bf16[4,64,4,128]{3,2,1,0:T(4,128)(2,1)} %copy-done.2, pred[64,32]{1,0:T(8,128)(4,1)S(1)} %iota_compare_fusion.1, bf16[64,32,512]{2,1,0:T(8,128)(2,1)} %param.17), kind=kOutput, calls=%fused_computation.56 | convolution fusion | flops 8485888 | bytes 2496512 | tf_op jit(solution)/shard_map/trhd,rchd->rhtc/dot_general | solution.py:29
  13.0 0.1 copy.89
  13.1 0.1 fusion.46
  13.3 0.1 copy.92
  13.4 0.7 fusion.35
  14.1 0.3 copy.90
  14.4 1.0 reshape.86
  15.5 0.4 fusion.38
  16.0 1.0 fusion.30
  16.9 0.1 copy.93
  17.2 0.1 copy.94
  17.4 58.3 %shard_map.127 = (bf16[4,2,2,16,3584]{4,3,2,1,0:T(8,128)(2,1)S(1)}, f32[2,16,1792]{2,1,0:T(8,128)S(1)}) custom-call(s32[1,1]{1,0:T(1,128)} %bitcast.1.flag_ref, bf16[256,512]{1,0:T(8,128)(2,1)S(1)} %bitcast.94, bf16[512,3584]{1,0:T(8,128)(2,1)} %proj_ref.1, bf16[16,7168]{1,0:T(8,128)(2,1)S(1)} %reshape.87.hidden_ref, f32[1,7168]{1,0:T(1,128)S(1)} %bitcast.95), custom_call_target="tpu_custom_call" | custom-call | tf_op jit(solution)/shard_map/pallas_call | solution.py:273
  75.7 5.1 %fusion.13 = bf16[1,256,1024]{2,1,0:T(8,128)(2,1)S(1)} fusion(bf16[256,3584]{1,0:T(8,128)(2,1)S(1)} %bitcast.96, bf16[3584,3,1024]{2,0,1:T(8,128)(2,1)} %bitcast.102), kind=kOutput, calls=%fused_computation.16 | convolution fusion | flops 1879310336 | bytes 9699328 | tf_op jit(solution)/shard_map/dot_general | solution.py:457
  80.9 5.1 %fusion.14 = bf16[1,256,1024]{2,1,0:T(8,128)(2,1)S(1)} fusion(bf16[256,3584]{1,0:T(8,128)(2,1)S(1)} %bitcast.97, bf16[3584,3,1024]{2,0,1:T(8,128)(2,1)} %bitcast.103), kind=kOutput, calls=%fused_computation.17 | convolution fusion | flops 1879310336 | bytes 9699328 | tf_op jit(solution)/shard_map/dot_general | solution.py:456
  86.0 1.1 pad_maximum_fusion
  87.3 0.1 select_reduce_fusion
  87.4 20.4 %all_gather.7 = f32[16,16,16]{2,1,0:T(8,128)S(1)} all-gather(f32[1,16,16]{2,1,0:T(8,128)S(1)} %bitcast.100), channel_id=1, replica_groups=mesh['rep'=2,'ep'=16] {'ep'}, dimensions={0}, use_global_device_ids=true | all-gather | bytes 17408 | tf_op jit(solution)/shard_map/all_gather | solution.py:423
  107.8 0.2 dynamic-slice_reduce_fusion
  108.1 1.6 reduce-scatter.2.cloned.1.call-done
  109.6 1.1 convert_element_type.31
  110.8 0.2 fusion.34
  110.9 8.9 %all_gather.6 = bf16[256,1024]{1,0:T(8,128)(2,1)S(1)} all-gather(bf16[128,1024]{1,0:T(8,128)(2,1)S(1)} %fusion.34), channel_id=1, replica_groups=mesh['rep'=2,'ep'=16] {'rep'}, dimensions={0}, use_global_device_ids=true | all-gather | bytes 786432 | tf_op jit(solution)/shard_map/all_gather | solution.py:461
  119.8 5.2 %fusion.4 = bf16[256,3584]{1,0:T(8,128)(2,1)S(1)} fusion(bf16[256,1024]{1,0:T(8,128)(2,1)S(1)} %all_gather.6, bf16[3584,3,1024]{2,0,1:T(8,128)(2,1)} %bitcast.104, f32[256]{0:T(256)S(1)} %mul.43), kind=kOutput, calls=%fused_computation.7 | convolution fusion | flops 1880883200 | bytes 9700352 | tf_op jit(solution)/shard_map/nf,df->nd/dot_general | solution.py:462
  125.0 42.4 %shard_map.128 = bf16[16,7168]{1,0:T(8,128)(2,1)S(1)} custom-call(s32[1,1]{1,0:T(1,128)} %bitcast.1.flag_ref, bf16[8,2,16,3584]{3,2,1,0:T(8,128)(2,1)S(1)} %bitcast.93, f32[2,16,1792]{2,1,0:T(8,128)S(1)} %get-tuple-element.8.residual_ref), custom_call_target="tpu_custom_call" | custom-call | tf_op jit(solution)/shard_map/pallas_call | solution.py:374
  167.5 0.1 reshape.90
  167.5 0.8 copy.135
  (27 shorter events, 0.5 us)
Async XLA Ops:
  6.5 9.4 %copy-start = (bf16[64,32,512]{2,1,0:T(8,128)(2,1)S(1)}, bf16[64,32,512]{2,1,0:T(8,128)(2,1)}, u32[]{:S(2)}) copy-start(bf16[64,32,512]{2,1,0:T(8,128)(2,1)} %param.18) | copy-start | bytes 6291460
  6.5 3.4 %copy-start.5 = (s32[64]{0:T(128)S(1)}, s32[64]{0:T(128)}, u32[]{:S(2)}) copy-start(s32[64]{0:T(128)} %param.19) | copy-start | bytes 772
  6.5 103.1 %reduce-scatter.2.cloned.1.call-start = ((), (), s32[]{:S(2)}) async-start(), calls=%async_computation.1 | async-start | bytes 1572864 | tf_op jit(solution)/shard_map/reduce_scatter | solution.py:459
  7.7 1.1 copy-start.2
  15.9 1.2 copy-start.7
  16.0 1.2 copy-start.3
  16.0 1.4 copy-start.1
  86.0 1.1 copy-start.6
  86.0 1.2 copy-start.4
Sparse Core Ops, SparseCore 0:
  87.3 22.3 reduce-scatter.1

commit v3 on v2

--- a/solution.py
+++ b/solution.py
@@ -12,7 +12,7 @@
 ROUTE_SCALE = 2.827
 EPSILON = 1e-06
 MESH = pl.DeviceIdType.MESH
-VMEM_BYTES = 48 * 1024 * 1024
+VMEM_BYTES = 60 * 1024 * 1024
 
 
 def attention(queries, new_keys, new_values, cache_keys, cache_values, cache_lengths):
@@ -148,15 +148,16 @@
     ]
 
 
-def dispatch_kernel(
+def layer_kernel(
     n_far,
     flag_ref,
     heads_ref,
     proj_ref,
     hidden_ref,
     gain_ref,
-    rows_ref,
-    residual_ref,
+    mix_ref,
+    weights_ref,
+    layer_ref,
     source,
     from_core,
     half,
@@ -164,22 +165,50 @@
     quarter,
     from_far,
     sems,
+    source2,
+    from_core2,
+    half2,
+    from_near2,
+    quarter2,
+    from_far2,
+    sems2,
     attended,
+    residual_ref,
     gathered,
     staged,
+    rows_ref,
+    weights,
+    hidden_sum,
+    sent_sum,
+    other_sum,
+    activated,
+    out_sum,
+    out_ref,
+    from_rep,
+    weight_sems,
     swap_sems,
     ring_sems,
     cross_sems,
+    sum_sems,
+    active_sems,
+    back_sems,
+    last_sems,
 ):
     f32, bf16 = jnp.float32, jnp.bfloat16
+    loads = [
+        pltpu.make_async_copy(weights_ref.at[i], weights.at[i], weight_sems.at[i])
+        for i in range(3)
+    ]
+    for load in loads:
+        load.start()
     spot = rep, far, near, core = place(4 * n_far)
     links = to_rep, to_core, to_near, others, to_far = neighbours(n_far, *spot)
     greet([to_rep, to_core, to_near] + to_far)
-    scatter = Scatter(
-        spot, links, source, from_core, half, from_near, quarter, from_far, sems
-    )
+    scatter = Scatter(spot, links, source, from_core, half, from_near, quarter, from_far, sems)
     own, piece = attended.shape[2], attended.shape[3]
     width = 4 * piece
+    chunk = piece // 2
+    count = 4 * n_far * own
 
     first = []
     for k in range(2):
@@ -201,9 +230,7 @@
         for copy in third[k]:
             copy.wait()
         attended[rep, k] = scatter.total(k).astype(bf16)
-        swaps.append(
-            send(attended.at[rep, k], attended.at[rep, k], swap_sems, (k,), to_rep)
-        )
+        swaps.append(send(attended.at[rep, k], attended.at[rep, k], swap_sems, (k,), to_rep))
     for copy in swaps:
         copy.wait()
 
@@ -222,24 +249,21 @@
         gathered[far, near, core, h] = (residual * scale * gain_ref[:, lanes]).astype(bf16)
 
     flag = flag_ref[0, 0]
-    mine = pl.ds(pl.multiple_of(rep * piece, 128), piece)
     pending = []
 
     def cross(f, n, c, index):
         low, high = gathered[f, n, c, 0], gathered[f, n, c, 1]
-        rows_ref[f, n, c, :, mine] = jnp.where(flag == 0, low, high)
+        rows_ref[rep, f, n, c] = jnp.where(flag == 0, low, high)
         staged[f, n, c] = jnp.where(flag == 0, high, low)
         pending.append(
-            send(staged.at[f, n, c], rows_ref.at[f, n, c, :, mine], cross_sems, (index,), to_rep)
+            send(staged.at[f, n, c], rows_ref.at[rep, f, n, c], cross_sems, (index,), to_rep)
         )
 
     def pass_on(f, n, c, index, device):
         block = gathered.at[f, n, c]
         return send(block, block, ring_sems, (index,), device)
 
-    far_copies = [
-        pass_on(far, near, core, d, device) for d, device in enumerate(to_far)
-    ]
+    far_copies = [pass_on(far, near, core, d, device) for d, device in enumerate(to_far)]
     base = n_far - 1
     for d in range(n_far):
         behind = lax.rem(far + n_far - d, n_far)
@@ -260,82 +284,108 @@
         other_copy.wait_send()
     for copy in far_copies:
         copy.wait_send()
+
+    tile = hidden_sum.shape[2] // 2
+
+    def products(q, t):
+        x = rows_ref[q].reshape(count, piece)
+        depth = pl.ds(pl.multiple_of(q * piece, 128), piece)
+        lanes = pl.ds(pl.multiple_of(t * tile, 128), tile)
+        gate = jnp.dot(x, weights[0, depth, lanes], preferred_element_type=f32)
+        up = jnp.dot(x, weights[1, depth, lanes], preferred_element_type=f32)
+        return gate, up
+
+    loads[0].wait()
+    loads[1].wait()
+
+    def own_piece(t, _):
+        gate, up = products(rep, t)
+        hidden_sum[t, :, :tile] = gate
+        hidden_sum[t, :, tile:] = up
+        return 0
+
+    lax.fori_loop(0, 4, own_piece, 0)
     for copy in pending:
         copy.wait()
-
-
-def dispatch(n_ep, flag, heads, projection, hidden, gain):
-    n_far = n_ep // 4
-    own, width = hidden.shape
-    piece = width // 4
-    bf16 = jnp.bfloat16
-    vmem = pl.BlockSpec(memory_space=pltpu.VMEM)
-    return pl.pallas_call(
-        functools.partial(dispatch_kernel, n_far),
-        out_shape=(
-            jax.ShapeDtypeStruct((n_far, 2, 2, own, 2 * piece), bf16),
-            jax.ShapeDtypeStruct((2, own, piece), jnp.float32),
-        ),
-        in_specs=[pl.BlockSpec(memory_space=pltpu.SMEM)] + [vmem] * 4,
-        out_specs=(vmem, vmem),
-        scratch_shapes=scatter_scratch(n_far, 2, (own, piece))
-        + [
-            pltpu.VMEM((2, 2, own, piece), bf16),
-            pltpu.VMEM((n_far, 2, 2, 2, own, piece), bf16),
-            pltpu.VMEM((n_far, 2, 2, own, piece), bf16),
-            pltpu.SemaphoreType.DMA((2, 2)),
-            pltpu.SemaphoreType.DMA((2, 4 * n_far - 1)),
-            pltpu.SemaphoreType.DMA((2, 4 * n_far)),
-        ],
-        compiler_params=pltpu.CompilerParams(
-            collective_id=0, has_side_effects=True, vmem_limit_bytes=VMEM_BYTES
-        ),
-    )(flag, heads, projection, hidden, gain)
-
-
-def combine_kernel(
-    n_far,
-    flag_ref,
-    out_ref,
-    residual_ref,
-    layer_ref,
-    source,
-    from_core,
-    half,
-    from_near,
-    quarter,
-    from_far,
-    sems,
-    from_rep,
-    cross_sems,
-    last_sems,
-):
-    spot = rep, far, near, core = place(4 * n_far)
-    links = to_rep, to_core, to_near, others, to_far = neighbours(n_far, *spot)
-    greet([to_rep, to_core, to_near] + to_far)
+    sums = []
+    for i in range(2):
+        t = 2 * (1 - rep) + i
+        gate, up = products(1 - rep, t)
+        sent_sum[i, :, :tile] = (hidden_sum[t, :, :tile] + gate).astype(bf16)
+        sent_sum[i, :, tile:] = (hidden_sum[t, :, tile:] + up).astype(bf16)
+        sums.append(send(sent_sum.at[i], other_sum.at[i], sum_sems, (i,), to_rep))
+
+    def other_piece(i, _):
+        t = 2 * rep + i
+        gate, up = products(1 - rep, t)
+        hidden_sum[t, :, :tile] += gate
+        hidden_sum[t, :, tile:] += up
+        return 0
+
+    lax.fori_loop(0, 2, other_piece, 0)
+    active = []
+    for i in range(2):
+        sums[i].wait()
+        t = 2 * rep + i
+        gate = hidden_sum[t, :, :tile] + other_sum[i, :, :tile].astype(f32)
+        up = hidden_sum[t, :, tile:] + other_sum[i, :, tile:].astype(f32)
+        activated[rep, i] = (gate / (1.0 + jnp.exp(-gate)) * up).astype(bf16)
+        active.append(
+            send(activated.at[rep, i], activated.at[rep, i], active_sems, (i,), to_rep)
+        )
+
+    def down(side, j):
+        total = jnp.zeros((count, chunk), f32)
+        for i in range(2):
+            rows = pl.ds(pl.multiple_of(j * chunk, 128), chunk)
+            lanes = pl.ds(pl.multiple_of((2 * side + i) * tile, 128), tile)
+            total += lax.dot_general(
+                activated[side, i],
+                weights[2, rows, lanes],
+                (((1,), (1,)), ((), ())),
+                preferred_element_type=f32,
+            )
+        return total
+
+    loads[2].wait()
+
+    def own_hidden(j, _):
+        out_sum[j] = down(rep, j)
+        return 0
+
+    lax.fori_loop(0, 4, own_hidden, 0)
+    for copy in active:
+        copy.wait()
+
+    def finish(j):
+        out = (out_sum[j] + down(1 - rep, j)) * mix_ref[...]
+        out_ref[j] = out.astype(bf16).reshape(2 * n_far, 2, own, chunk)
+
+    back = []
+    for k in range(2):
+        finish(2 * (1 - rep) + k)
+        back.append(
+            send(out_ref.at[2 * (1 - rep) + k], from_rep.at[k], back_sems, (k,), to_rep)
+        )
+
+    def finish_own(k, _):
+        finish(2 * rep + k)
+        return 0
+
+    lax.fori_loop(0, 2, finish_own, 0)
+
     scatter = Scatter(
-        spot, links, source, from_core, half, from_near, quarter, from_far, sems
-    )
-    piece = residual_ref.shape[2]
-    chunk = piece // 2
-    flag = flag_ref[0, 0]
-
-    def lanes(owner, k):
-        return pl.ds(pl.multiple_of(owner * piece + k * chunk, 128), chunk)
-
-    crossing = [
-        send(out_ref.at[:, :, :, lanes(1 - rep, k)], from_rep.at[k], cross_sems, (k,), to_rep)
-        for k in range(2)
-    ]
+        spot, links, source2, from_core2, half2, from_near2, quarter2, from_far2, sems2
+    )
     first = []
     for k in range(2):
-        crossing[k].wait()
+        back[k].wait()
 
         def arrange(j, _):
-            mine = out_ref[j // 2, j % 2, :, lanes(rep, k)]
+            mine = out_ref[2 * rep + k, j // 2, j % 2]
             other = from_rep[k, j // 2, j % 2]
-            source[k, j // 2, j % 2, 0] = jnp.where(flag == 0, mine, other)
-            source[k, j // 2, j % 2, 1] = jnp.where(flag == 0, other, mine)
+            source2[k, j // 2, j % 2, 0] = jnp.where(flag == 0, mine, other)
+            source2[k, j // 2, j % 2, 1] = jnp.where(flag == 0, other, mine)
             return 0
 
         lax.fori_loop(0, 4 * n_far, arrange, 0)
@@ -354,38 +404,62 @@
         for copy in third[k]:
             copy.wait()
         layer = residual_ref[:, :, k * chunk : (k + 1) * chunk] + scatter.total(k)
-        layer = layer.astype(jnp.bfloat16)
+        layer = layer.astype(bf16)
         for h in range(2):
-            spot_lanes = pl.ds(
-                pl.multiple_of((2 * h + rep) * piece + k * chunk, 128), chunk
-            )
-            layer_ref[:, spot_lanes] = layer[h]
-            block = layer_ref.at[:, spot_lanes]
+            lanes = pl.ds(pl.multiple_of((2 * h + rep) * piece + k * chunk, 128), chunk)
+            layer_ref[:, lanes] = layer[h]
+            block = layer_ref.at[:, lanes]
             last.append(send(block, block, last_sems, (2 * k + h,), to_rep))
     for copy in last:
         copy.wait()
 
 
-def combine(n_ep, flag, out, residual):
+def layer(n_ep, flag, heads, projection, hidden, gain, mix, weights):
     n_far = n_ep // 4
-    _, own, piece = residual.shape
-    bf16 = jnp.bfloat16
+    own, width = hidden.shape
+    piece = width // 4
+    chunk = piece // 2
+    count = n_ep * own
+    units = weights.shape[2]
+    tile = units // 4
+    f32, bf16 = jnp.float32, jnp.bfloat16
     vmem = pl.BlockSpec(memory_space=pltpu.VMEM)
     return pl.pallas_call(
-        functools.partial(combine_kernel, n_far),
-        out_shape=jax.ShapeDtypeStruct((own, 4 * piece), bf16),
-        in_specs=[pl.BlockSpec(memory_space=pltpu.SMEM)] + [vmem] * 2,
+        functools.partial(layer_kernel, n_far),
+        out_shape=jax.ShapeDtypeStruct((own, width), bf16),
+        in_specs=[pl.BlockSpec(memory_space=pltpu.SMEM)]
+        + [vmem] * 5
+        + [pl.BlockSpec(memory_space=pl.ANY)],
         out_specs=vmem,
-        scratch_shapes=scatter_scratch(n_far, 2, (2, own, piece // 2))
+        scratch_shapes=scatter_scratch(n_far, 2, (own, piece))
+        + scatter_scratch(n_far, 2, (2, own, chunk))
         + [
-            pltpu.VMEM((2, 2 * n_far, 2, own, piece // 2), bf16),
+            pltpu.VMEM((2, 2, own, piece), bf16),
+            pltpu.VMEM((2, own, piece), f32),
+            pltpu.VMEM((n_far, 2, 2, 2, own, piece), bf16),
+            pltpu.VMEM((n_far, 2, 2, own, piece), bf16),
+            pltpu.VMEM((2, n_far, 2, 2, own, piece), bf16),
+            pltpu.VMEM(weights.shape, bf16),
+            pltpu.VMEM((4, count, 2 * tile), f32),
+            pltpu.VMEM((2, count, 2 * tile), bf16),
+            pltpu.VMEM((2, count, 2 * tile), bf16),
+            pltpu.VMEM((2, 2, count, tile), bf16),
+            pltpu.VMEM((4, count, chunk), f32),
+            pltpu.VMEM((4, 2 * n_far, 2, own, chunk), bf16),
+            pltpu.VMEM((2, 2 * n_far, 2, own, chunk), bf16),
+            pltpu.SemaphoreType.DMA((3,)),
+            pltpu.SemaphoreType.DMA((2, 2)),
+            pltpu.SemaphoreType.DMA((2, 4 * n_far - 1)),
+            pltpu.SemaphoreType.DMA((2, 4 * n_far)),
+            pltpu.SemaphoreType.DMA((2, 2)),
+            pltpu.SemaphoreType.DMA((2, 2)),
             pltpu.SemaphoreType.DMA((2, 2)),
             pltpu.SemaphoreType.DMA((2, 4)),
         ],
         compiler_params=pltpu.CompilerParams(
-            collective_id=1, has_side_effects=True, vmem_limit_bytes=VMEM_BYTES
+            collective_id=0, has_side_effects=True, vmem_limit_bytes=VMEM_BYTES
         ),
-    )(flag, out.reshape(2 * n_far, 2, own, 2 * piece), residual)
+    )(flag, heads, projection, hidden, gain, mix, weights)
 
 
 def on_device(
@@ -426,33 +500,40 @@
     heads = attention(queries, new_keys, new_values, cache_keys, cache_values, cache_lengths)
     heads = heads.reshape(n_ep * own, -1)
     hidden = hidden_in.transpose(1, 0, 2).reshape(own, width)
+    weights = expert_sectioned[0]
     by_kernel = n_rep == 2 and n_ep % 4 == 0 and own % 16 == 0 and half % 512 == 0
-    if by_kernel:
+    if by_kernel and weights.shape[2] % 512 == 0:
         flag = (owners[0] != me_rep).astype(jnp.int32).reshape(1, 1)
-        arrived, residual = dispatch(n_ep, flag, heads, out_sectioned, hidden, norm_gain[None])
-        arrived = arrived.reshape(n_ep * own, half)
-    else:
-        partial = jnp.dot(heads, out_sectioned, preferred_element_type=f32).astype(bf16)
-        summed = lax.psum_scatter(partial, "ep", scatter_dimension=0, tiled=True)
-        swapped = lax.all_to_all(
-            summed.reshape(n_rep, part, half), "rep", split_axis=0, concat_axis=0, tiled=True
-        )
-        attended = swapped.transpose(1, 0, 2).reshape(part, width)
-        hidden = lax.dynamic_slice_in_dim(hidden, me_rep * part, part, 0)
-        residual = hidden.astype(f32) + attended.astype(f32)
-        mean_square = jnp.mean(residual * residual, axis=1, keepdims=True)
-        normalized = (residual * lax.rsqrt(mean_square + EPSILON) * norm_gain).astype(bf16)
-
-        gathered = lax.all_gather(normalized, "ep", axis=0, tiled=True)
-        blocks = gathered.reshape(n_ep * part, n_rep, half).transpose(1, 0, 2)
-        blocks = jnp.take(blocks, bucket_of, axis=0)
-        arrived = lax.all_to_all(blocks, "rep", split_axis=0, concat_axis=0, tiled=True)
-        arrived = arrived.reshape(n_rep * n_ep * part, half)
-
-        mix = mix.reshape(n_ep, n_rep, part).transpose(1, 0, 2)
+        out = layer(
+            n_ep,
+            flag,
+            heads,
+            out_sectioned,
+            hidden,
+            norm_gain[None],
+            mix.reshape(-1, 1),
+            weights.transpose(1, 0, 2),
+        )
+        return out.reshape(row_block, steps, width).transpose(1, 0, 2)
+    partial = jnp.dot(heads, out_sectioned, preferred_element_type=f32).astype(bf16)
+    summed = lax.psum_scatter(partial, "ep", scatter_dimension=0, tiled=True)
+    swapped = lax.all_to_all(
+        summed.reshape(n_rep, part, half), "rep", split_axis=0, concat_axis=0, tiled=True
+    )
+    attended = swapped.transpose(1, 0, 2).reshape(part, width)
+    hidden = lax.dynamic_slice_in_dim(hidden, me_rep * part, part, 0)
+    residual = hidden.astype(f32) + attended.astype(f32)
+    mean_square = jnp.mean(residual * residual, axis=1, keepdims=True)
+    normalized = (residual * lax.rsqrt(mean_square + EPSILON) * norm_gain).astype(bf16)
+
+    gathered = lax.all_gather(normalized, "ep", axis=0, tiled=True)
+    blocks = gathered.reshape(n_ep * part, n_rep, half).transpose(1, 0, 2)
+    blocks = jnp.take(blocks, bucket_of, axis=0)
+    arrived = lax.all_to_all(blocks, "rep", split_axis=0, concat_axis=0, tiled=True)
+    arrived = arrived.reshape(n_rep * n_ep * part, half)
+
+    mix = mix.reshape(n_ep, n_rep, part).transpose(1, 0, 2)
     mix = mix.reshape(-1, 1)
-
-    weights = expert_sectioned[0]
     gate = jnp.dot(arrived, weights[:, 0], preferred_element_type=f32).astype(bf16)
     up = jnp.dot(arrived, weights[:, 1], preferred_element_type=f32).astype(bf16)
     both = jnp.stack([gate, up])
@@ -462,17 +543,14 @@
     out = jnp.einsum("nf,df->nd", activated, weights[:, 2], preferred_element_type=f32)
     out = (out * mix).astype(bf16)
 
-    if by_kernel:
-        layer = combine(n_ep, flag, out, residual)
-        return layer.reshape(row_block, steps, width).transpose(1, 0, 2)
     back = lax.all_to_all(
         out.reshape(n_rep, n_ep * part, half), "rep", split_axis=0, concat_axis=0, tiled=True
     )
     back = jnp.take(back, owners, axis=0).transpose(1, 0, 2).reshape(n_ep * part, width)
     routed = lax.psum_scatter(back, "ep", scatter_dimension=0, tiled=True)
-    layer = (residual + routed.astype(f32)).astype(bf16)
-    layer = lax.all_gather(layer, "rep", axis=0, tiled=True)
-    return layer.reshape(row_block, steps, width).transpose(1, 0, 2)
+    result = (residual + routed.astype(f32)).astype(bf16)
+    result = lax.all_gather(result, "rep", axis=0, tiled=True)
+    return result.reshape(row_block, steps, width).transpose(1, 0, 2)
 
 
 def solution(mesh):

time: 176 us -> 155 us (0.88)
  Pallas kernels: 101 us -> 115 us
  matrix products: 20.3 us -> 6.54 us
  between operations: 13.7 us -> 1.01 us
  blocking collectives: 29.3 us -> 23.4 us
  other arithmetic: 3.72 us -> 1.33 us
    dot_general x3 -> x0, matrix products: 15.5 us -> none  [the longest x1 5.18 us: on_device(): jnp.einsum('nf,df->nd', activated, weights[:, 2], preferred_element_type=...]
    pallas_call x2 -> x1, Pallas kernels: 101 us -> 115 us  [layer(): pl.pallas_call(functools.partial(layer_kernel, n_far), out_shape=jax.Shap...]
    all_gather x1 -> x0, blocking collectives: 8.89 us -> none  [on_device(): activated = lax.all_gather(activated, 'rep', axis=0, tiled=True)]
    all_gather x1, blocking collectives: 20.4 us -> 23.4 us  [on_device(): mix = lax.all_gather(dense, 'ep', axis=0, tiled=False)]
  transfers between devices with their start and end apart: 1 -> 0, of which waited for: 1 -> 0; matrix products, arithmetic and copies ran while one was open for 0% -> 0% of each run, Pallas kernels for 0% -> 0%
where the time goes in v3:
time: 155 us
  Pallas kernels  115 us (74%)
  blocking collectives  23.4 us (15%)
  local copies, waits for them, and re-layouts  7.4 us (5%)
  matrix products  6.54 us (4%)
    pallas_call x1, Pallas kernels, layer(): pl.pallas_call(functools.partial(layer_kernel, n_far), out_shape=jax.Shap...  115 us
    all_gather x1, blocking collectives, on_device(): mix = lax.all_gather(dense, 'ep', axis=0, tiled=False)  23.4 us

profile of v3, /device:TPU:0, one launch (start us, length us, event | category | flops | bytes accessed | tf_op | source)
XLA Modules:
  0.0 154.5 jit_solution(217937539015023214)
XLA Ops:
  0.8 1.0 reshape.79
  1.8 1.0 reshape.77
  2.9 0.4 fusion.29
  3.3 0.3 copy.91
  3.6 0.1 iota_compare_fusion.1
  3.7 0.0 copy-start.1
  3.7 2.9 %fusion.39 = (f32[64,4,4]{2,1,0:T(4,128)S(1)}, f32[64,4,4,32]{3,2,1,0:T(4,128)S(1)}) fusion(bf16[4,64,4,128]{3,2,1,0:T(4,128)(2,1)S(1)} %reshape.77, pred[64,32]{1,0:T(8,128)(4,1)S(1)} %iota_compare_fusion.1, bf16[64,32,512]{2,1,0:T(8,128)(2,1)} %param.17), kind=kOutput, calls=%fused_computation.39 | convolution fusion | flops 8485888 | bytes 2496512 | tf_op jit(solution)/shard_map/trhd,rchd->rhtc/dot_general | solution.py:29
  6.7 0.1 fusion.34
  6.8 0.1 copy.92
  7.0 0.1 copy.94
  7.1 0.1 fusion.35
  7.2 0.3 copy.95
  7.5 0.1 reshape.81
  7.6 1.2 fusion.27
  8.8 0.7 fusion.24
  9.6 0.1 copy.97
  9.7 0.0 copy-start.2
  9.8 0.0 copy-start.5
  9.8 1.9 %fusion.21 = bf16[64,4,4,128]{3,1,2,0:T(4,128)(2,1)S(1)} fusion(f32[64,4,4,128]{3,2,1,0:T(4,128)} %fusion.27, f32[64,4,4,32]{3,2,1,0:T(4,128)S(1)} %get-tuple-element.8, f32[64,4,4]{1,2,0:T(4,128)S(1)} %add_bitcast_fusion, f32[64,4,4]{2,1,0:T(4,128)S(1)} %max.8, bf16[64,32,512]{2,1,0:T(8,128)(2,1)S(1)} %copy-done), kind=kOutput, calls=%fused_computation.11 | convolution fusion | flops 8847360 | bytes 3022848 | tf_op jit(solution)/shard_map/rhtc,rchd->rhtd/dot_general | solution.py:39
  11.7 0.0 copy-start.3
  11.7 0.1 copy.98
  11.8 0.7 copy.140
  12.6 0.1 copy.99
  12.7 0.7 reshape.82.hidden_ref
  13.5 0.1 multiply_divide_fusion
  13.5 0.0 copy-done.3
  13.6 0.1 select_reduce_fusion
  13.7 23.4 %all_gather.3 = f32[16,16,16]{2,1,0:T(8,128)S(1)} all-gather(f32[1,16,16]{2,1,0:T(8,128)S(1)} %bitcast.62), channel_id=1, replica_groups=mesh['rep'=2,'ep'=16] {'ep'}, dimensions={0}, use_global_device_ids=true | all-gather | bytes 17408 | tf_op jit(solution)/shard_map/all_gather | solution.py:497
  37.1 0.8 constant_dynamic-slice_fusion
  37.9 114.8 %shard_map.127 = bf16[16,7168]{1,0:T(8,128)(2,1)} custom-call(s32[1,1]{1,0:T(1,128)} %bitcast.1.flag_ref, bf16[256,512]{1,0:T(8,128)(2,1)} %bitcast.57, bf16[512,3584]{1,0:T(8,128)(2,1)} %proj_ref.1, bf16[16,7168]{1,0:T(8,128)(2,1)} %reshape.82.hidden_ref, f32[1,7168]{1,0:T(1,128)} %bitcast.63, f32[256,1]{1,0:T(8,128)} %bitcast.59, ...), custom_call_target="tpu_custom_call" | custom-call | tf_op jit(solution)/shard_map/pallas_call | solution.py:427
  152.7 1.0 reshape.84
  153.7 0.8 copy.141
  (11 shorter events, 0.1 us)
Async XLA Ops:
  0.0 9.7 %copy-start = (bf16[64,32,512]{2,1,0:T(8,128)(2,1)S(1)}, bf16[64,32,512]{2,1,0:T(8,128)(2,1)}, u32[]{:S(2)}) copy-start(bf16[64,32,512]{2,1,0:T(8,128)(2,1)} %param.18) | copy-start | bytes 6291460
  0.0 3.6 %copy-start.4 = (s32[64]{0:T(128)S(1)}, s32[64]{0:T(128)}, u32[]{:S(2)}) copy-start(s32[64]{0:T(128)} %param.19) | copy-start | bytes 772
  3.7 3.8 %copy-start.1 = (bf16[4,64,512]{2,1,0:T(8,128)(2,1)S(1)}, bf16[4,64,512]{2,1,0:T(8,128)(2,1)}, u32[]{:S(2)}) copy-start(bf16[4,64,512]{2,1,0:T(8,128)(2,1)} %param.16) | copy-start | bytes 786436
  9.7 2.8 %copy-start.2 = (bf16[4,4,7168]{2,1,0:T(4,128)(2,1)S(1)}, bf16[4,4,7168]{2,1,0:T(4,128)(2,1)}, u32[]{:S(2)}) copy-start(bf16[4,4,7168]{2,1,0:T(4,128)(2,1)} %param.13) | copy-start | bytes 688132
  9.8 3.7 %copy-start.5 = (f32[4,4,8]{2,1,0:T(4,128)S(1)}, f32[4,4,8]{2,1,0:T(4,128)}, u32[]{:S(2)}) copy-start(f32[4,4,8]{2,1,0:T(4,128)} %param.21) | copy-start | bytes 1540
  11.7 1.8 %copy-start.3 = (s32[4,4,8]{2,1,0:T(4,128)S(1)}, s32[4,4,8]{2,1,0:T(4,128)}, u32[]{:S(2)}) copy-start(s32[4,4,8]{2,1,0:T(4,128)} %param.20) | copy-start | bytes 1540

commit v4 on v3

--- a/solution.py
+++ b/solution.py
@@ -155,7 +155,7 @@
     proj_ref,
     hidden_ref,
     gain_ref,
-    mix_ref,
+    share_ref,
     weights_ref,
     layer_ref,
     source,
@@ -193,6 +193,8 @@
     active_sems,
     back_sems,
     last_sems,
+    shares,
+    share_sems,
 ):
     f32, bf16 = jnp.float32, jnp.bfloat16
     loads = [
@@ -210,6 +212,15 @@
     chunk = piece // 2
     count = 4 * n_far * own
 
+    shares[far, near, core] = share_ref[...]
+
+    def pass_shares(index, device, block):
+        return send(block, block, share_sems, (index,), device)
+
+    share_far = [
+        pass_shares(d, device, shares.at[far, near, core]) for d, device in enumerate(to_far)
+    ]
+
     first = []
     for k in range(2):
         product = jnp.dot(
@@ -221,10 +232,15 @@
     for k in range(2):
         first[k].wait()
         second.append(scatter.second(k))
+    for copy in share_far:
+        copy.wait()
+    share_near = pass_shares(n_far - 1, to_near, shares.at[:, near, core])
     third = []
     for k in range(2):
         second[k].wait()
         third.append(scatter.third(k))
+    share_near.wait()
+    share_core = pass_shares(n_far, to_core, shares.at[:, :, core])
     swaps = []
     for k in range(2):
         for copy in third[k]:
@@ -348,6 +364,12 @@
         return total
 
     loads[2].wait()
+    share_core.wait()
+    every = shares[...].reshape(count, shares.shape[4])
+    expert = lax.broadcasted_iota(jnp.int32, every.shape, 1)
+    mix = jnp.sum(
+        jnp.where(expert == 4 * far + 2 * near + core, every, 0.0), axis=1, keepdims=True
+    )
 
     def own_hidden(j, _):
         out_sum[j] = down(rep, j)
@@ -358,7 +380,7 @@
         copy.wait()
 
     def finish(j):
-        out = (out_sum[j] + down(1 - rep, j)) * mix_ref[...]
+        out = (out_sum[j] + down(1 - rep, j)) * mix
         out_ref[j] = out.astype(bf16).reshape(2 * n_far, 2, own, chunk)
 
     back = []
@@ -393,8 +415,8 @@
         if k == 0:
             first[0].wait()
             second = [scatter.second(0)]
-    second[0].wait()
-    third = [scatter.third(0)]
+            second[0].wait()
+            third = [scatter.third(0)]
     first[1].wait()
     second.append(scatter.second(1))
     second[1].wait()
@@ -414,7 +436,7 @@
         copy.wait()
 
 
-def layer(n_ep, flag, heads, projection, hidden, gain, mix, weights):
+def layer(n_ep, flag, heads, projection, hidden, gain, share, weights):
     n_far = n_ep // 4
     own, width = hidden.shape
     piece = width // 4
@@ -455,11 +477,13 @@
             pltpu.SemaphoreType.DMA((2, 2)),
             pltpu.SemaphoreType.DMA((2, 2)),
             pltpu.SemaphoreType.DMA((2, 4)),
+            pltpu.VMEM((n_far, 2, 2) + share.shape, f32),
+            pltpu.SemaphoreType.DMA((2, n_far + 1)),
         ],
         compiler_params=pltpu.CompilerParams(
             collective_id=0, has_side_effects=True, vmem_limit_bytes=VMEM_BYTES
         ),
-    )(flag, heads, projection, hidden, gain, mix, weights)
+    )(flag, heads, projection, hidden, gain, share, weights)
 
 
 def on_device(
@@ -494,8 +518,6 @@
     experts = jnp.arange(n_ep, dtype=jnp.int32)
     dense = jnp.sum(jnp.where(expert_ids[..., None] == experts, share[..., None], 0.0), axis=2)
     dense = dense.transpose(1, 0, 2).reshape(own, n_ep)
-    mix = lax.all_gather(dense, "ep", axis=0, tiled=False)
-    mix = lax.dynamic_index_in_dim(mix, me_ep, axis=2, keepdims=False)
 
     heads = attention(queries, new_keys, new_values, cache_keys, cache_values, cache_lengths)
     heads = heads.reshape(n_ep * own, -1)
@@ -511,7 +533,7 @@
             out_sectioned,
             hidden,
             norm_gain[None],
-            mix.reshape(-1, 1),
+            jnp.pad(dense, ((0, 0), (0, -n_ep % 128))),
             weights.transpose(1, 0, 2),
         )
         return out.reshape(row_block, steps, width).transpose(1, 0, 2)
@@ -532,6 +554,8 @@
     arrived = lax.all_to_all(blocks, "rep", split_axis=0, concat_axis=0, tiled=True)
     arrived = arrived.reshape(n_rep * n_ep * part, half)
 
+    mix = lax.all_gather(dense, "ep", axis=0, tiled=False)
+    mix = lax.dynamic_index_in_dim(mix, me_ep, axis=2, keepdims=False)
     mix = mix.reshape(n_ep, n_rep, part).transpose(1, 0, 2)
     mix = mix.reshape(-1, 1)
     gate = jnp.dot(arrived, weights[:, 0], preferred_element_type=f32).astype(bf16)

time: 155 us -> 137 us (0.88)
  blocking collectives: 23.4 us -> 0 us
  Pallas kernels: 115 us -> 120 us
    all_gather x1 -> x0, blocking collectives: 23.4 us -> none  [on_device(): mix = lax.all_gather(dense, 'ep', axis=0, tiled=False)]
    pallas_call x1, Pallas kernels: 115 us -> 120 us  [layer(): pl.pallas_call(functools.partial(layer_kernel, n_far), out_shape=jax.Shap...]
where the time goes in v4:
time: 137 us; the launch traced here: 136 us
  Pallas kernels  120 us (88%)
  local copies, waits for them, and re-layouts  7.25 us (5%)
  matrix products  6.54 us (5%)
    pallas_call x1, Pallas kernels, layer(): pl.pallas_call(functools.partial(layer_kernel, n_far), out_shape=jax.Shap...  120 us
    dot_general x1, matrix products, attention(): jnp.einsum('trhd,rchd->rhtc', q, keys_old, preferred_element_type=f32)  2.94 us

profile of v4, /device:TPU:0, one launch (start us, length us, event | category | flops | bytes accessed | tf_op | source)
XLA Modules:
  0.0 136.4 jit_solution(13238467122834440985)
XLA Ops:
  0.0 0.0 copy-start
  0.8 1.0 reshape.78
  1.8 1.0 reshape.76
  2.9 0.4 fusion.29
  3.3 0.3 copy.66
  3.7 0.1 iota_compare_fusion.1
  3.7 0.0 copy-start.1
  3.7 2.9 %fusion.39 = (f32[64,4,4]{2,1,0:T(4,128)S(1)}, f32[64,4,4,32]{3,2,1,0:T(4,128)S(1)}) fusion(bf16[4,64,4,128]{3,2,1,0:T(4,128)(2,1)S(1)} %reshape.76, pred[64,32]{1,0:T(8,128)(4,1)S(1)} %iota_compare_fusion.1, bf16[64,32,512]{2,1,0:T(8,128)(2,1)} %param.17), kind=kOutput, calls=%fused_computation.38 | convolution fusion | flops 8485888 | bytes 2496512 | tf_op jit(solution)/shard_map/trhd,rchd->rhtc/dot_general | solution.py:29
  6.7 0.1 fusion.34
  6.8 0.1 copy.67
  7.0 0.1 copy.69
  7.1 0.1 fusion.35
  7.2 0.3 copy.70
  7.5 0.1 reshape.80
  7.6 1.2 fusion.27
  8.8 0.7 fusion.24
  9.6 0.1 copy.72
  9.7 0.0 copy-start.2
  9.8 0.0 copy-start.5
  9.8 1.9 %fusion.21 = bf16[64,4,4,128]{3,1,2,0:T(4,128)(2,1)S(1)} fusion(f32[64,4,4,128]{3,2,1,0:T(4,128)} %fusion.27, f32[64,4,4,32]{3,2,1,0:T(4,128)S(1)} %get-tuple-element.8, f32[64,4,4]{1,2,0:T(4,128)S(1)} %add_bitcast_fusion, f32[64,4,4]{2,1,0:T(4,128)S(1)} %max.8, bf16[64,32,512]{2,1,0:T(8,128)(2,1)S(1)} %copy-done), kind=kOutput, calls=%fused_computation.11 | convolution fusion | flops 8847360 | bytes 3022848 | tf_op jit(solution)/shard_map/rhtc,rchd->rhtd/dot_general | solution.py:39
  11.7 0.0 copy-start.3
  11.7 0.1 copy.73
  11.8 0.7 copy.114
  12.6 0.1 copy.74
  12.7 0.7 reshape.81.hidden_ref
  13.5 0.1 multiply_divide_fusion
  13.5 0.0 copy-done.3
  13.6 0.1 select_reduce_fusion
  13.7 0.6 pad.4.share_ref
  14.3 120.2 %shard_map.127 = bf16[16,7168]{1,0:T(8,128)(2,1)} custom-call(s32[1,1]{1,0:T(1,128)} %bitcast.1.flag_ref, bf16[256,512]{1,0:T(8,128)(2,1)} %bitcast.56, bf16[512,3584]{1,0:T(8,128)(2,1)} %proj_ref.1, bf16[16,7168]{1,0:T(8,128)(2,1)} %reshape.81.hidden_ref, f32[1,7168]{1,0:T(1,128)} %bitcast.61, f32[16,128]{1,0:T(8,128)} %pad.4.share_ref, ...), custom_call_target="tpu_custom_call" | custom-call | tf_op jit(solution)/shard_map/pallas_call | solution.py:449
  134.5 1.0 reshape.83
  135.6 0.8 copy.115
  (10 shorter events, 0.1 us)
Async XLA Ops:
  0.0 9.7 %copy-start = (bf16[64,32,512]{2,1,0:T(8,128)(2,1)S(1)}, bf16[64,32,512]{2,1,0:T(8,128)(2,1)}, u32[]{:S(2)}) copy-start(bf16[64,32,512]{2,1,0:T(8,128)(2,1)} %param.18) | copy-start | bytes 6291460
  0.0 3.6 %copy-start.4 = (s32[64]{0:T(128)S(1)}, s32[64]{0:T(128)}, u32[]{:S(2)}) copy-start(s32[64]{0:T(128)} %param.19) | copy-start | bytes 772
  3.7 3.8 %copy-start.1 = (bf16[4,64,512]{2,1,0:T(8,128)(2,1)S(1)}, bf16[4,64,512]{2,1,0:T(8,128)(2,1)}, u32[]{:S(2)}) copy-start(bf16[4,64,512]{2,1,0:T(8,128)(2,1)} %param.16) | copy-start | bytes 786436
  9.7 2.8 %copy-start.2 = (bf16[4,4,7168]{2,1,0:T(4,128)(2,1)S(1)}, bf16[4,4,7168]{2,1,0:T(4,128)(2,1)}, u32[]{:S(2)}) copy-start(bf16[4,4,7168]{2,1,0:T(4,128)(2,1)} %param.13) | copy-start | bytes 688132
  9.8 3.7 %copy-start.5 = (f32[4,4,8]{2,1,0:T(4,128)S(1)}, f32[4,4,8]{2,1,0:T(4,128)}, u32[]{:S(2)}) copy-start(f32[4,4,8]{2,1,0:T(4,128)} %param.21) | copy-start | bytes 1540
  11.7 1.8 %copy-start.3 = (s32[4,4,8]{2,1,0:T(4,128)S(1)}, s32[4,4,8]{2,1,0:T(4,128)}, u32[]{:S(2)}) copy-start(s32[4,4,8]{2,1,0:T(4,128)} %param.20) | copy-start | bytes 1540
